TPU v7x, 32 devices: a whole 2x2x4 slice. The times are simulated.
32 devices in a mesh: tm: 8 (over z, y), mod: 4 (over x, core).
Axes of the slice: x: 2, y: 2, z: 4, core: 2. Of those that a mesh axis runs over, the one named last changes fastest.
Arguments:
- filterbank: bfloat16 [1024, 128], P('tm'), may hold values from -6 to 6
- conv_weight: bfloat16 [384, 1280], replicated, may hold values from -0.3125 to 0.3125
- mlp_gain: float32 [1280], replicated, may hold values from 0.25 to 1.75
- up_weight: bfloat16 [1280, 5120], P('tm', 'mod'), may hold values from -0.15625 to 0.15625
- down_weight: bfloat16 [5120, 1280], P('mod', 'tm'), may hold values from -0.078125 to 0.078125
- post_gain: float32 [1280], replicated, may hold values from 0.25 to 1.75
- audio_weight: bfloat16 [1280, 1792], P(None, 'mod'), may hold values from -0.15625 to 0.15625
- patches: bfloat16 [2048, 1280], P('tm'), may hold values from -6 to 6
- vision_gain: float32 [1280], replicated, may hold values from 0.25 to 1.75
- vision_weight: bfloat16 [5120, 1792], P('tm', 'mod'), may hold values from -0.078125 to 0.078125
- retention: int32 [8, 64], P('tm'), may hold values from 0 to 63, each once within a row
- kept_count: int32 [8], P('tm'), may hold values from 1 to 64, 256 in all
Outputs:
- sequence: bfloat16 [8, 96, 1792], P('tm', None, 'mod')
Inputs may be any that keep to these rules, and one draw needn't show every extreme that they name: `retention`: each row lists every merged token of its frame once. `kept_count`: the counts sum to 256.
All inputs are finite; a program needn't handle non-finite values. No bound on the sum of `kept_count` on one device may be relied on, other than what follows from the above.
Results may differ from a plain program's by a relative error of at most 0.01.
Values may be sent and summed in bfloat16 or wider, within the bound.
A program may use at most 64 MiB of HBM per device.

v0:
```python
import jax
import jax.numpy as jnp
from jax import lax
from jax.sharding import PartitionSpec as P

MRG_FRAME = 64
AUD_TOK = 64
SEQ_DEV = 96


def carried_in(value, axis, join, neutral):
    count, mine = (lax.axis_size(axis), lax.axis_index(axis))
    pieces = lax.all_gather(value, axis)
    running = jnp.full_like(value, 0) + jnp.asarray(neutral, value.dtype)

    def hop(position, running):
        longer = join(running, pieces[position])
        return jnp.where(position < mine, longer, running)

    return lax.fori_loop(0, count - 1, hop, running)


def padded(shard, sides, width):
    for axis, dim in sides:
        peers, length = (lax.axis_size(axis), shard.shape[dim])
        up = [(i, (i + 1) % peers) for i in range(peers - 1)]
        down = [(j, i) for i, j in up]
        last = lax.slice_in_dim(shard, length - width, length, axis=dim)
        first = lax.slice_in_dim(shard, 0, width, axis=dim)
        before = lax.ppermute(last, axis, up)
        after = lax.ppermute(first, axis, down)
        shard = jnp.concatenate([before, shard, after], axis=dim)
    return shard


def layer_norm(values, scale_gain):
    average = jnp.mean(values, axis=-1, keepdims=True)
    centred = values - average
    variance = jnp.mean(centred * centred, axis=-1, keepdims=True)
    return centred * lax.rsqrt(variance + 1e-05) * scale_gain


def rms_norm(values, scale_gain):
    square_mean = jnp.mean(values * values, axis=-1, keepdims=True)
    return values * lax.rsqrt(square_mean + 1e-06) * scale_gain


def pool_pairs(values):
    return values.reshape(-1, 2, values.shape[-1]).mean(axis=1)


def add_counts(earlier, later):
    return earlier + later


def on_device(
    filterbank,
    conv_weight,
    mlp_gain,
    up_weight,
    down_weight,
    post_gain,
    audio_weight,
    patches,
    vision_gain,
    vision_weight,
    retention,
    kept_count,
):
    placed = kept_count + AUD_TOK
    starts = carried_in(placed, "tm", add_counts, jnp.zeros((1,), jnp.int32))
    framed = padded(filterbank, (("tm", 0),), 1)
    unfolded = jnp.concatenate([framed[:-2], framed[1:-1], framed[2:]], axis=1)
    stem = jax.nn.gelu(
        jnp.dot(unfolded, conv_weight, preferred_element_type=jnp.float32), approximate=False
    ).astype(jnp.bfloat16)
    residual = stem.astype(jnp.float32)
    hidden = layer_norm(residual, mlp_gain).astype(jnp.bfloat16)
    up_share = lax.all_gather(up_weight, "tm", axis=0, tiled=True)
    pre_act = jnp.dot(hidden, up_share, preferred_element_type=jnp.float32)
    activated = jax.nn.gelu(pre_act, approximate=False).astype(jnp.bfloat16)
    down_share = lax.all_gather(down_weight, "tm", axis=1, tiled=True)
    partial_value = jnp.dot(activated, down_share, preferred_element_type=jnp.float32)
    pooled_share = lax.psum_scatter(
        pool_pairs(partial_value).astype(jnp.bfloat16), "mod", scatter_dimension=0, tiled=True
    ).astype(jnp.float32)
    share_rows = pooled_share.shape[0]
    own_rows = lax.dynamic_slice_in_dim(
        pool_pairs(residual), lax.axis_index("mod") * share_rows, share_rows, 0
    )
    share_normed = layer_norm(own_rows + pooled_share, post_gain).astype(jnp.bfloat16)
    normed = lax.all_gather(share_normed, "mod", axis=0, tiled=True)
    audio_tokens = jnp.dot(normed, audio_weight, preferred_element_type=jnp.float32).astype(
        jnp.bfloat16
    )
    patch_normed = rms_norm(patches.astype(jnp.float32), vision_gain).astype(jnp.bfloat16)
    merged = patch_normed.reshape(-1, 4 * patch_normed.shape[1])
    vision_share = lax.all_gather(vision_weight, "tm", axis=0, tiled=True)
    visual_tokens = jnp.dot(merged, vision_share, preferred_element_type=jnp.float32).astype(
        jnp.bfloat16
    )
    peer_count = lax.axis_size("tm")
    per_peer = (AUD_TOK + MRG_FRAME + peer_count - 1) // peer_count
    kept_here = kept_count[0]
    first_slot = starts[0]
    all_tokens = jnp.concatenate([visual_tokens, audio_tokens], axis=0)
    peer_ids = jnp.arange(peer_count, dtype=jnp.int32)[:, None]
    round_ids = jnp.arange(per_peer, dtype=jnp.int32)[None, :]
    local_index = round_ids * peer_count + (peer_ids - first_slot) % peer_count
    valid_rows = local_index < kept_here + AUD_TOK
    kept_index = jnp.take(retention[0], jnp.minimum(local_index, MRG_FRAME - 1), axis=0)
    source_index = jnp.where(
        local_index < kept_here, kept_index, MRG_FRAME + local_index - kept_here
    )
    source_index = jnp.where(valid_rows, source_index, 0).astype(jnp.int32)
    send_rows = jnp.take(all_tokens, source_index.reshape(-1), axis=0).reshape(
        peer_count, per_peer, all_tokens.shape[1]
    )
    send_slots = jnp.where(valid_rows, (first_slot + local_index) // peer_count, SEQ_DEV).astype(
        jnp.int32
    )
    recv_rows, recv_slots = (
        lax.all_to_all(send_rows, "tm", split_axis=0, concat_axis=0, tiled=True),
        lax.all_to_all(send_slots, "tm", split_axis=0, concat_axis=0, tiled=True),
    )
    sequence = jnp.zeros((SEQ_DEV, all_tokens.shape[1]), jnp.bfloat16)
    sequence = sequence.at[recv_slots.reshape(-1)].set(
        recv_rows.reshape(-1, all_tokens.shape[1]), mode="drop"
    )
    return sequence[None]


def solution(mesh):
    return jax.shard_map(
        on_device,
        mesh=mesh,
        in_specs=(
            P("tm", None),
            P(),
            P(),
            P("tm", "mod"),
            P("mod", "tm"),
            P(),
            P(None, "mod"),
            P("tm", None),
            P(),
            P("tm", "mod"),
            P("tm", None),
            P("tm"),
        ),
        out_specs=P("tm", None, "mod"),
        check_vma=False,
    )
```

profile of v0, /device:TPU:0, one launch (start us, length us, event | category | flops | bytes accessed | tf_op | source)
XLA Modules:
  0.0 267.4 jit_solution(14068031621403169184)
XLA Ops:
  8.8 4.9 %collective-permute-start = (bf16[1,128]{1,0:T(2,128)(2,1)S(1)}, bf16[1,128]{1,0:T(2,128)(2,1)S(1)}, u32[]{:S(2)}, u32[]{:S(2)}) collective-permute-start(bf16[1,128]{1,0:T(2,128)(2,1)S(1)} %get-tuple-element.93), channel_id=1, source_target_pairs={{0,4},{4,8},{8,12},{12,16},{16,20},{20,24},{24,28},{1,5},{5,9},{9,... | collective-permute-start | bytes 776 | tf_op jit(solution)/shard_map/ppermute | solution.py:30
  13.6 1.3 collective-permute-start.1
  15.0 4.1 %collective-permute-done.1 = bf16[1,128]{1,0:T(2,128)(2,1)S(1)} collective-permute-done((bf16[1,128]{1,0:T(2,128)(2,1)S(1)}, bf16[1,128]{1,0:T(2,128)(2,1)S(1)}, u32[]{:S(2)}, u32[]{:S(2)}) %collective-permute-start.1) | collective-permute-done | bytes 288 | tf_op jit(solution)/shard_map/ppermute | solution.py:31
  19.1 3.0 %convert_reduce_fusion = (f32[128]{0:T(128)S(1)}, bf16[128,1280]{1,0:T(8,128)(2,1)S(1)}) fusion(bf16[384,1280]{1,0:T(8,128)(2,1)} %param.15, bf16[1,128]{1,0:T(2,128)(2,1)S(1)} %collective-permute-done.1, bf16[128,128]{1,0:T(8,128)(2,1)} %param.14, bf16[1,128]{1,0:T(2,128)(2,1)S(1)} %collective-permute-done), kind=kOutput, calls=%fused_computation.51 | convolution fusion | flops 137297792 | bytes 1344512 | tf_op jit(solution)/shard_map/dot_general | solution.py:75
  22.4 51.8 %all-gather.7.cloned.1.call-done = bf16[1280,1280]{1,0:T(8,128)(2,1)} async-done(((bf16[160,1280]{1,0:T(8,128)(2,1)}), bf16[1280,1280]{1,0:T(8,128)(2,1)}) %all-gather.7.cloned.1.call-update) | async-done | bytes 3276816 | tf_op jit(solution)/shard_map/all_gather | solution.py:79
  74.2 62.8 %all-gather.9.cloned.1.call-done = bf16[1280,1280]{0,1:T(8,128)(2,1)} async-done(((bf16[1280,160]{0,1:T(8,128)(2,1)}), bf16[1280,1280]{0,1:T(8,128)(2,1)}) %all-gather.9.cloned.1.call-update) | async-done | bytes 3276816 | tf_op jit(solution)/shard_map/all_gather | solution.py:82
  136.9 5.7 %fusion.23 = f32[128,1280]{1,0:T(8,128)S(1)} fusion(bf16[1280,1280]{0,1:T(8,128)(2,1)} %all-gather.9.cloned.1.call-done, bf16[1280,1280]{1,0:T(8,128)(2,1)} %all-gather.7.cloned.1.call-done, bf16[128,1280]{1,0:T(8,128)(2,1)S(1)} %get-tuple-element.98, f32[1280]{0:T(1024)S(1)} %copy-done.5, f32[128]{0:T(128)S(1)} %add_rsqrt_fusion.2, ...), kind=kOutput, calls=%fused_computation.52 | convolution fusion | flops 850329600 | bytes 7542784 | tf_op jit(solution)/shard_map/dot_general | solution.py:83
  143.1 0.8 reduce_sum.67
  147.1 9.9 %all-reduce = s32[8]{0:T(128)S(1)} all-reduce(s32[8]{0:T(128)S(1)} %add_dynamic-update-slice_fusion), channel_id=2, replica_groups=mesh['tm'=8,'mod'=4] {'tm'}, use_global_device_ids=true, to_apply=%add | all-reduce | flops 8 | bytes 64
  157.0 9.1 %while.13 = (s32[]{:T(128)}, s32[1]{0:T(128)}, s32[]{:T(128)}, s32[8,1]{0,1:T(1,128)S(1)}, s32[]{:T(128)}) while((s32[]{:T(128)}, s32[1]{0:T(128)}, s32[]{:T(128)}, s32[8,1]{0,1:T(1,128)S(1)}, s32[]{:T(128)}) %tuple.42), condition=%wide.region_1.2_spmd, body=%wide.region_0.1_spmd.sunk | while | flops 5 | bytes 107 | solution.py:20
  166.9 3.3 %all-to-all-start = ((s32[8,1,16]{2,1,0:T(1,128)}), s32[8,1,16]{2,1,0:T(1,128)S(1)}, u32[]{:S(2)}, u32[]{:S(2)}) async-start(s32[8,1,16]{2,1,0:T(1,128)} %get-tuple-element.96), calls=%async_computation | async-start | bytes 8192 | tf_op jit(solution)/shard_map/all_to_all | solution.py:124
  170.7 1.2 gather_fusion
  173.3 0.8 reduce_sum.64
  174.1 2.4 all-to-all-done
  177.8 0.9 fusion.75
  178.7 1.0 multiply_reduce_fusion.1
  179.7 0.9 multiply_convert_fusion.7
  180.6 5.5 %all_gather.23 = bf16[64,1280]{1,0:T(8,128)(2,1)S(1)} all-gather(bf16[16,1280]{1,0:T(8,128)(2,1)S(1)} %multiply_convert_fusion.7), channel_id=1, replica_groups=mesh['tm'=8,'mod'=4] {'mod'}, dimensions={0}, use_global_device_ids=true | all-gather | bytes 204800 | tf_op jit(solution)/shard_map/all_gather | solution.py:92
  186.6 56.6 %all-gather.5.cloned.1.call-done = bf16[5120,448]{0,1:T(8,128)(2,1)} async-done(((bf16[640,448]{0,1:T(8,128)(2,1)}), bf16[5120,448]{0,1:T(8,128)(2,1)}) %all-gather.5.cloned.1.call-update) | async-done | bytes 4587536 | tf_op jit(solution)/shard_map/all_gather | solution.py:98
  243.2 3.8 %convolution_convert_fusion.1 = bf16[64,448]{1,0:T(8,128)(2,1)S(1)} fusion(bf16[64,5120]{1,0:T(8,128)(2,1)S(1)} %reshape.397, bf16[5120,448]{0,1:T(8,128)(2,1)} %all-gather.5.cloned.1.call-done), kind=kOutput, calls=%fused_computation.10 | convolution fusion | flops 293629952 | bytes 5300224 | tf_op jit(solution)/shard_map/dot_general | solution.py:99
  247.0 0.8 gather_fusion.1
  248.5 3.4 %all-to-all-start.1 = ((bf16[8,16,448]{2,1,0:T(8,128)(2,1)}), bf16[8,16,448]{2,1,0:T(8,128)(2,1)S(1)}, u32[]{:S(2)}, u32[]{:S(2)}) async-start(bf16[8,16,448]{2,1,0:T(8,128)(2,1)} %broadcast_select_fusion), calls=%async_computation.2 | async-start | bytes 262144 | tf_op jit(solution)/shard_map/all_to_all | solution.py:123
  251.9 7.3 %all-to-all-done.1 = bf16[8,16,448]{2,1,0:T(8,128)(2,1)S(1)} async-done(((bf16[8,16,448]{2,1,0:T(8,128)(2,1)}), bf16[8,16,448]{2,1,0:T(8,128)(2,1)S(1)}, u32[]{:S(2)}, u32[]{:S(2)}) %all-to-all-start.1) | async-done | bytes 114720 | tf_op jit(solution)/shard_map/all_to_all | solution.py:123
  259.2 1.6 scatter_custom_fusion
  (69 shorter events, 15.0 us)
Async XLA Ops:
  6.5 179.6 %copy-start = (bf16[1280,448]{0,1:T(8,128)(2,1)S(1)}, bf16[1280,448]{0,1:T(8,128)(2,1)}, u32[]{:S(2)}) copy-start(bf16[1280,448]{0,1:T(8,128)(2,1)} %param.20) | copy-start | bytes 3440644
  6.5 67.6 %all-gather.7.cloned.1.call-start = ((), (), s32[]{:S(2)}) async-start(), calls=%async_computation.4 | async-start | bytes 3686400 | tf_op jit(solution)/shard_map/all_gather | solution.py:79
  7.3 129.7 %all-gather.9.cloned.1.call-start = ((), (), s32[]{:S(2)}) async-start(), calls=%async_computation.5 | async-start | bytes 3686400 | tf_op jit(solution)/shard_map/all_gather | solution.py:82
  8.0 169.8 %reduce-scatter.2.cloned.1.call-start = ((), (), s32[]{:S(2)}) async-start(), calls=%async_computation.6 | async-start | bytes 204800 | tf_op jit(solution)/shard_map/reduce_scatter | solution.py:84
  8.8 6.2 %collective-permute-start = (bf16[1,128]{1,0:T(2,128)(2,1)S(1)}, bf16[1,128]{1,0:T(2,128)(2,1)S(1)}, u32[]{:S(2)}, u32[]{:S(2)}) collective-permute-start(bf16[1,128]{1,0:T(2,128)(2,1)S(1)} %get-tuple-element.93), channel_id=1, source_target_pairs={{0,4},{4,8},{8,12},{12,16},{16,20},{20,24},{24,28},{1,5},{5,9},{9,... | collective-permute-start | bytes 776 | tf_op jit(solution)/shard_map/ppermute | solution.py:30
  13.6 123.3 %copy-start.5 = (f32[1280]{0:T(1024)S(1)}, f32[1280]{0:T(1024)}, u32[]{:S(2)}) copy-start(f32[1280]{0:T(1024)} %param.16) | copy-start | bytes 15364
  13.6 5.4 %collective-permute-start.1 = (bf16[1,128]{1,0:T(2,128)(2,1)S(1)}, bf16[1,128]{1,0:T(2,128)(2,1)S(1)}, u32[]{:S(2)}, u32[]{:S(2)}) collective-permute-start(bf16[1,128]{1,0:T(2,128)(2,1)S(1)} %get-tuple-element.94), channel_id=1, source_target_pairs={{4,0},{8,4},{12,8},{16,12},{20,16},{24,20},{28,24},{5,1},{9,5},{13... | collective-permute-start | bytes 776 | tf_op jit(solution)/shard_map/ppermute | solution.py:31
  142.6 3.2 %copy-start.6 = (u32[32]{0:T(128)S(1)}, u32[32]{0:T(128)}, u32[]{:S(2)}) copy-start(u32[32]{0:T(128)} %constant.188) | copy-start | bytes 388
  142.6 28.1 %copy-start.1 = (s32[1,64]{1,0:T(1,128)S(1)}, s32[1,64]{1,0:T(1,128)}, u32[]{:S(2)}) copy-start(s32[1,64]{1,0:T(1,128)} %param.24) | copy-start | bytes 772
  143.0 29.0 %copy-start.2 = (bf16[256,1280]{1,0:T(8,128)(2,1)S(1)}, bf16[256,1280]{1,0:T(8,128)(2,1)}, u32[]{:S(2)}) copy-start(bf16[256,1280]{1,0:T(8,128)(2,1)} %param.21) | copy-start | bytes 1966084
  143.8 28.5 %copy-start.3 = (f32[1280]{0:T(1024)S(1)}, f32[1280]{0:T(1024)}, u32[]{:S(2)}) copy-start(f32[1280]{0:T(1024)} %param.22) | copy-start | bytes 15364
  144.6 98.6 %all-gather.5.cloned.1.call-start = ((), (), s32[]{:S(2)}) async-start(), calls=%async_computation.3 | async-start | bytes 5160960 | tf_op jit(solution)/shard_map/all_gather | solution.py:98
  166.9 9.6 %all-to-all-start = ((s32[8,1,16]{2,1,0:T(1,128)}), s32[8,1,16]{2,1,0:T(1,128)S(1)}, u32[]{:S(2)}, u32[]{:S(2)}) async-start(s32[8,1,16]{2,1,0:T(1,128)} %get-tuple-element.96), calls=%async_computation | async-start | bytes 8192 | tf_op jit(solution)/shard_map/all_to_all | solution.py:124
  171.9 7.8 %copy-start.4 = (f32[1280]{0:T(1024)S(1)}, f32[1280]{0:T(1024)}, u32[]{:S(2)}) copy-start(f32[1280]{0:T(1024)} %param.19) | copy-start | bytes 15364
  248.5 10.7 %all-to-all-start.1 = ((bf16[8,16,448]{2,1,0:T(8,128)(2,1)}), bf16[8,16,448]{2,1,0:T(8,128)(2,1)S(1)}, u32[]{:S(2)}, u32[]{:S(2)}) async-start(bf16[8,16,448]{2,1,0:T(8,128)(2,1)} %broadcast_select_fusion), calls=%async_computation.2 | async-start | bytes 262144 | tf_op jit(solution)/shard_map/all_to_all | solution.py:123
Sparse Core Ops, SparseCore 0:
  9.5 64.5 all-gather.6
  76.4 60.5 all-gather.8
  144.7 18.2 reduce-scatter.1
  165.0 78.0 all-gather.4
where the time goes:
time: 268 us; the launch traced here: 267 us
  waiting for transfers between devices  187 us (70%)
  blocking collectives  15.4 us (6%)
  between operations  14.1 us (5%)
  matrix products  13 us (5%)
  starting transfers between devices  12.9 us (5%)
  local copies, waits for them, and re-layouts  11.7 us (4%)
  other arithmetic  8.72 us (3%)
  loops' own time  4.59 us (2%)
    all_gather x1, waiting for transfers between devices, on_device(): down_share = lax.all_gather(down_weight, 'tm', axis=1, tiled=True)  62.8 us
    all_gather x1, waiting for transfers between devices, on_device(): vision_share = lax.all_gather(vision_weight, 'tm', axis=0, tiled=True)  56.6 us
    all_gather x1, waiting for transfers between devices, on_device(): up_share = lax.all_gather(up_weight, 'tm', axis=0, tiled=True)  51.8 us
    unnamed x1, blocking collectives  9.89 us
    all_to_all x1, waiting for transfers between devices, on_device(): lax.all_to_all(send_rows, 'tm', split_axis=0, concat_axis=0, tiled=True)  7.27 us
    dot_general x1, matrix products, on_device(): jnp.dot(activated, down_share, preferred_element_type=jnp.float32)  5.68 us
    all_gather x1, blocking collectives, on_device(): normed = lax.all_gather(share_normed, 'mod', axis=0, tiled=True)  5.52 us
  transfers between devices with their start and end apart: 8, of which 6 were waited for; matrix products, arithmetic and copies ran while one was open for 7% of the time, Pallas kernels for 0%

commit v1 on v0

--- a/solution.py
+++ b/solution.py
@@ -1,6 +1,8 @@
 import jax
 import jax.numpy as jnp
 from jax import lax
+from jax.experimental import pallas as pl
+from jax.experimental.pallas import tpu as pltpu
 from jax.sharding import PartitionSpec as P
 
 MRG_FRAME = 64
@@ -130,9 +132,293 @@
     return sequence[None]
 
 
+F32, BF16, I32 = jnp.float32, jnp.bfloat16, jnp.int32
+MESH = pl.DeviceIdType.MESH
+TM, MOD = 8, 4
+
+
+def iota(shape, dim):
+    return lax.broadcasted_iota(I32, shape, dim)
+
+
+def onehot(mask, value=1.0):
+    return jnp.where(mask, value, 0.0).astype(BF16)
+
+
+def mm(a, b):
+    return lax.dot_general(a, b, (((1,), (0,)), ((), ())), preferred_element_type=F32)
+
+
+def mm_nt(a, b):
+    return lax.dot_general(a, b, (((1,), (1,)), ((), ())), preferred_element_type=F32)
+
+
+def mm_tn(a, b):
+    return lax.dot_general(a, b, (((0,), (0,)), ((), ())), preferred_element_type=F32)
+
+
+def gelu(x):
+    return 0.5 * x * (1.0 + lax.erf(x * 0.7071067811865476))
+
+
+FB, META, WGT, MRG, VIS, TOT, FWD, NRM, COR, XAX = 0, 7, 14, 21, 28, 35, 42, 45, 48, 49
+N_SEM = 50
+
+
+def fused_kernel(
+    fb, conv, gain1, up, dn, gain2, aud_w, pat, gain_v, vis_w, ret, kept, out,
+    fbp, meta_s, meta, w_s, w_r, m_s, x_r, v_s, v_r, stem, hid, pa, own,
+    a_s, a_r, b_s, b_r, c_s, c_r, nrm, send_sem, recv_sem,
+):
+    me = lax.axis_index("tm")
+    mo = lax.axis_index("mod")
+    xx, cc = mo // 2, mo % 2
+    tm_peers = [lax.rem(me + d, TM) for d in range(1, TM)]
+    mod_peers = [lax.rem(mo + d, MOD) for d in range(1, MOD)]
+    core_peer = xx * 2 + (1 - cc)
+    x_peer = (1 - xx) * 2 + cc
+
+    barrier = pltpu.get_barrier_semaphore()
+    for peer in tm_peers:
+        pl.semaphore_signal(barrier, inc=1, device_id={"tm": peer}, device_id_type=MESH)
+    for peer in mod_peers:
+        pl.semaphore_signal(barrier, inc=1, device_id={"mod": peer}, device_id_type=MESH)
+
+    def copy(src, dst, slot, to):
+        c = pltpu.make_async_remote_copy(
+            src_ref=src, dst_ref=dst, send_sem=send_sem.at[slot], recv_sem=recv_sem.at[slot],
+            device_id=to, device_id_type=MESH,
+        )
+        c.start()
+        return c
+
+    def to_tm(src_of, dst, base):
+        return [copy(src_of(p), dst, base + d, {"tm": p}) for d, p in enumerate(tm_peers)]
+
+    def arrive(copies):
+        for c in copies:
+            c.wait_recv()
+
+    fbp[0:16] = jnp.zeros((16, 128), BF16)
+    fbp[1040:1056] = jnp.zeros((16, 128), BF16)
+    my_rows = pl.ds(pl.multiple_of(16 + me * 128, 16), 128)
+    fbp[my_rows, :] = fb[...]
+    hit = ret[...] == iota((64, 64), 0)
+    inv = jnp.sum(jnp.where(hit, iota((64, 64), 1).astype(F32), 0.0), axis=1, keepdims=True)
+    kept_f = kept[...].astype(F32)
+    inv = jnp.where(inv < kept_f, inv, -4096.0)
+    meta_s[0:64] = jnp.broadcast_to(inv, (64, 128))
+    meta_s[64:72] = jnp.broadcast_to(kept_f, (8, 128))
+    meta[me] = meta_s[...]
+
+    pl.semaphore_wait(barrier, TM + MOD - 2)
+    fb_copies = to_tm(lambda p: fb, fbp.at[my_rows], FB)
+    meta_copies = to_tm(lambda p: meta_s, meta.at[me], META)
+
+    row, col = iota((512, 128), 0), iota((512, 128), 1)
+    for t in range(TM):
+        w_s[t, 0:160] = up[:, 128 * t : 128 * t + 128]
+        w_s[t, 160:320] = dn[:, 128 * t : 128 * t + 128]
+    for g in range(2):
+        lanes = slice(1024 + 128 * g, 1152 + 128 * g)
+        rest = jnp.concatenate(
+            [up[0:80, lanes], up[80:160, lanes], dn[0:80, lanes], dn[80:160, lanes]], axis=1
+        )
+        for a in range(4):
+            pick = onehot((row // 128 == col // 32) & (row % 128 == 32 * a + col % 32))
+            w_s[4 * g + a, 320:400] = mm(rest, pick).astype(BF16)
+    w_copies = to_tm(lambda p: w_s.at[p], w_r.at[me], WGT)
+    w_r[me] = w_s[me]
+
+    pv = pat[pl.ds(pl.multiple_of(mo * 64, 64), 64), :].astype(F32)
+    ms = jnp.sum(pv * pv, axis=1, keepdims=True) * (1.0 / 1280.0)
+    pn = (pv * lax.rsqrt(ms + 1e-06) * gain_v[...]).astype(BF16)
+    r64, c64 = iota((64, 64), 0), iota((64, 64), 1)
+    pn = mm(onehot(c64 == 4 * (r64 % 16) + r64 // 16), pn).astype(BF16)
+    for t in range(TM):
+        q, h = t // 2, t % 2
+        m_s[t] = pn[16 * q : 16 * q + 16, 640 * h : 640 * h + 640]
+    m_copies = to_tm(lambda p: m_s.at[p], x_r.at[mo, me], MRG)
+    x_r[mo, me] = m_s[me]
+
+    arrive(fb_copies)
+
+    def stem_step(s, carry):
+        base = pl.multiple_of(s * 128, 128)
+        rows = fbp[pl.ds(base, 160), :].astype(F32)
+        taps = jnp.concatenate([rows[15:143], rows[16:144], rows[17:145]], axis=1).astype(BF16)
+        st = gelu(mm(taps, conv[...])).astype(BF16)
+        stem[pl.ds(base, 128), :] = st
+        v = st.astype(F32)
+        v = v - jnp.sum(v, axis=1, keepdims=True) * (1.0 / 1280.0)
+        var = jnp.sum(v * v, axis=1, keepdims=True) * (1.0 / 1280.0)
+        hid[pl.ds(base, 128), :] = (v * lax.rsqrt(var + 1e-05) * gain1[...]).astype(BF16)
+        return carry
+
+    lax.fori_loop(0, 4, stem_step, 0)
+    arrive(m_copies)
+    x_copies = [
+        copy(x_r.at[mo], x_r.at[mo], FWD + d, {"mod": p}) for d, p in enumerate(mod_peers)
+    ]
+    lax.fori_loop(4, 8, stem_step, 0)
+
+    arrive(meta_copies)
+    ends, before, running = [], [], jnp.zeros((1, 128), F32)
+    for s in range(TM):
+        before.append(running)
+        running = running + meta[s, 64:65, :]
+        ends.append(running.astype(I32))
+
+    arrive(w_copies)
+    rem = jnp.concatenate([w_r[t, 320:400] for t in range(TM)], axis=0)
+    ri, ci = iota((128, 512), 0), iota((128, 512), 1)
+    rem = mm(rem, onehot((ci % 128 < 32) & (ri == 32 * (ci // 128) + ci % 128))).astype(BF16)
+
+    def assemble(first, lane):
+        main = jnp.concatenate([w_r[t, first : first + 160] for t in range(TM)], axis=0)
+        parts = []
+        for t in range(TM):
+            parts.append(rem[80 * t : 80 * t + 80, lane : lane + 128])
+            parts.append(rem[80 * t : 80 * t + 80, lane + 128 : lane + 256])
+        return jnp.concatenate([main, jnp.concatenate(parts, axis=0)], axis=1)
+
+    up_all = assemble(0, 0)
+    dn_all = assemble(160, 256)
+
+    def pool_rows(holder, r_s2, r_q, frames, span_ends):
+        blocks = []
+        for h in range(2):
+            j = 8 * r_q + ((holder - span_ends[h]) & 7)
+            blocks.append(onehot((r_s2 == h) & (frames // 2 == j), 0.5))
+        return jnp.concatenate(blocks, axis=1)
+
+    r128, c128 = iota((128, 128), 0), iota((128, 128), 1)
+    for p in range(MOD):
+        act = gelu(mm(hid[256 * p : 256 * p + 256], up_all)).astype(BF16)
+        pool = pool_rows(r128 // 16, (r128 // 8) % 2, r128 % 8, c128, ends[2 * p : 2 * p + 2])
+        pa[p % 2, p // 2] = mm(pool, act).astype(BF16)
+
+    a_s[...] = mm_nt(pa[1 - cc].reshape(256, 256), dn_all).astype(BF16).reshape(2, 128, 1280)
+    a_copy = copy(a_s, a_r, COR, {"mod": core_peer})
+    own[...] = mm_nt(pa[cc].reshape(256, 256), dn_all).reshape(2, 128, 1280)
+    a_copy.wait_recv()
+    b_s[...] = (own[1 - xx] + a_r[1 - xx].astype(F32)).astype(BF16)
+    b_copy = copy(b_s, b_r, XAX, {"mod": x_peer})
+
+    arrive(x_copies)
+    pos = jnp.concatenate(
+        [meta[t, 16 * m : 16 * m + 16, :] + before[t] for m in range(MOD) for t in range(TM)], axis=0
+    )
+    pos = jnp.concatenate([pos, pos], axis=1).astype(I32)
+    lane = iota((512, 256), 1)
+    pick = onehot(pos == 8 * (lane % 32) + lane // 32)
+    chosen = mm_tn(pick, x_r[...].reshape(512, 640)).astype(BF16)
+    v_s[...] = mm_nt(chosen, vis_w[...]).astype(BF16).reshape(TM, 32, 448)
+
+    b_copy.wait_recv()
+    total = own[xx] + a_r[xx].astype(F32) + b_r[...].astype(F32)
+    c_s[...] = total.astype(BF16).reshape(TM, 16, 1280)
+    c_copies = to_tm(lambda p: c_s.at[p], c_r.at[me], TOT)
+    v_copies = to_tm(lambda p: v_s.at[p], v_r.at[me], VIS)
+    c_r[me] = c_s[me]
+    v_r[me] = v_s[me]
+
+    r16, c16 = iota((16, 128), 0), iota((16, 128), 1)
+    mine = []
+    for h in range(2):
+        e = jnp.zeros((1, 128), I32)
+        for p in range(MOD):
+            e = jnp.where(mo == p, ends[2 * p + h], e)
+        mine.append(e)
+    pool = pool_rows(me, r16 // 8, r16 % 8, c16, mine)
+    pooled = mm(pool, stem[pl.ds(pl.multiple_of(mo * 256, 256), 256), :])
+
+    lane = iota((1, 128), 1)
+    g = 8 * lane + me
+    v_slot = lane
+    a_slot = jnp.zeros((1, 128), I32)
+    for s in range(TM):
+        v_slot = v_slot + jnp.where(ends[s] <= g, 8, 0)
+        j = 8 * (lane % 8) + ((me - ends[s]) & 7)
+        a_slot = jnp.where((lane - 32) // 8 == s, ((ends[s] + j) >> 3) + 8 * s, a_slot)
+    slot = jnp.where(lane < 32, v_slot, jnp.where(lane < 96, a_slot, -1))
+    place = onehot(slot == iota((96, 128), 0))
+
+    arrive(c_copies)
+    for t in range(TM):
+        pooled = pooled + c_r[t].astype(F32)
+    v = pooled - jnp.sum(pooled, axis=1, keepdims=True) * (1.0 / 1280.0)
+    var = jnp.sum(v * v, axis=1, keepdims=True) * (1.0 / 1280.0)
+    nrm[mo] = (v * lax.rsqrt(var + 1e-05) * gain2[...]).astype(BF16)
+    n_copies = [copy(nrm.at[mo], nrm.at[mo], NRM + d, {"mod": p}) for d, p in enumerate(mod_peers)]
+
+    arrive(v_copies)
+    visual = v_r[0].astype(F32)
+    for t in range(1, TM):
+        visual = visual + v_r[t].astype(F32)
+    arrive(n_copies)
+    audio = mm_nt(nrm[...].reshape(64, 1280), aud_w[...])
+    tokens = jnp.concatenate(
+        [visual.astype(BF16), audio.astype(BF16), jnp.zeros((32, 448), BF16)], axis=0
+    )
+    out[...] = mm(place, tokens).astype(BF16)
+
+    for group in (fb_copies, meta_copies, w_copies, m_copies, x_copies, v_copies, c_copies, n_copies):
+        for c in group:
+            c.wait_send()
+    a_copy.wait_send()
+    b_copy.wait_send()
+
+
+def on_device_fused(
+    filterbank, conv_weight, mlp_gain, up_weight, down_weight, post_gain, audio_weight,
+    patches, vision_gain, vision_weight, retention, kept_count,
+):
+    vm = pl.BlockSpec(memory_space=pltpu.VMEM)
+    scratch = [
+        pltpu.VMEM((1056, 128), BF16),
+        pltpu.VMEM((72, 128), F32),
+        pltpu.VMEM((TM, 72, 128), F32),
+        pltpu.VMEM((TM, 400, 128), BF16),
+        pltpu.VMEM((TM, 400, 128), BF16),
+        pltpu.VMEM((TM, 16, 640), BF16),
+        pltpu.VMEM((MOD, TM, 16, 640), BF16),
+        pltpu.VMEM((TM, 32, 448), BF16),
+        pltpu.VMEM((TM, 32, 448), BF16),
+        pltpu.VMEM((1024, 1280), BF16),
+        pltpu.VMEM((1024, 1280), BF16),
+        pltpu.VMEM((2, 2, 128, 256), BF16),
+        pltpu.VMEM((2, 128, 1280), F32),
+        pltpu.VMEM((2, 128, 1280), BF16),
+        pltpu.VMEM((2, 128, 1280), BF16),
+        pltpu.VMEM((128, 1280), BF16),
+        pltpu.VMEM((128, 1280), BF16),
+        pltpu.VMEM((TM, 16, 1280), BF16),
+        pltpu.VMEM((TM, 16, 1280), BF16),
+        pltpu.VMEM((MOD, 16, 1280), BF16),
+        pltpu.SemaphoreType.DMA((N_SEM,)),
+        pltpu.SemaphoreType.DMA((N_SEM,)),
+    ]
+    sequence = pl.pallas_call(
+        fused_kernel,
+        out_shape=jax.ShapeDtypeStruct((SEQ_DEV, vision_weight.shape[1]), BF16),
+        in_specs=[vm] * 12,
+        out_specs=vm,
+        scratch_shapes=scratch,
+        compiler_params=pltpu.CompilerParams(
+            collective_id=0, has_side_effects=True, vmem_limit_bytes=56 * 1024 * 1024
+        ),
+    )(
+        filterbank, conv_weight, mlp_gain[None], up_weight, down_weight.T, post_gain[None],
+        audio_weight.T, patches, vision_gain[None], vision_weight.T, retention, kept_count[None],
+    )
+    return sequence[None]
+
+
 def solution(mesh):
+    fused = mesh.shape["tm"] == TM and mesh.shape["mod"] == MOD
     return jax.shard_map(
-        on_device,
+        on_device_fused if fused else on_device,
         mesh=mesh,
         in_specs=(
             P("tm", None),

time: 268 us -> 80 us (0.30)
  waiting for transfers between devices: 187 us -> 0 us
  Pallas kernels: 0 us -> 72.8 us
  blocking collectives: 15.4 us -> 0 us
  between operations: 14.1 us -> 0.66 us
  matrix products: 13 us -> 0 us
  starting transfers between devices: 12.9 us -> 0 us
  other arithmetic: 8.72 us -> 0 us
  local copies, waits for them, and re-layouts: 11.7 us -> 5.43 us
  loops' own time: 4.59 us -> 0 us
    all_gather x3 -> x0, waiting for transfers between devices: 171 us -> none  [the longest x1 62.8 us: on_device(): down_share = lax.all_gather(down_weight, 'tm', axis=1, tiled=True)]
    pallas_call x0 -> x1, Pallas kernels: none -> 72.8 us  [on_device_fused(): pl.pallas_call(fused_kernel, out_shape=jax.ShapeDtypeStruct((SEQ_DEV, vis...]
    dot_general x4 -> x0, matrix products: 13 us -> none  [the longest x1 5.68 us: on_device(): jnp.dot(activated, down_share, preferred_element_type=jnp.float32)]
    unnamed x1 -> x0, blocking collectives: 9.89 us -> none
    all_to_all x2 -> x0, waiting for transfers between devices: 9.69 us -> none  [the longest x1 7.27 us: on_device(): lax.all_to_all(send_rows, 'tm', split_axis=0, concat_axis=0, tiled=True)]
    all_to_all x2 -> x0, starting transfers between devices: 6.68 us -> none  [the longest x1 3.37 us: on_device(): lax.all_to_all(send_rows, 'tm', split_axis=0, concat_axis=0, tiled=True)]
    ppermute x2 -> x0, starting transfers between devices: 6.15 us -> none  [the longest x1 4.86 us: padded(): before = lax.ppermute(last, axis, up)]
    all_gather x1 -> x0, blocking collectives: 5.52 us -> none  [on_device(): normed = lax.all_gather(share_normed, 'mod', axis=0, tiled=True)]
  transfers between devices with their start and end apart: 8 -> 0, of which waited for: 6 -> 0; matrix products, arithmetic and copies ran while one was open for 7% -> 0% of each run, Pallas kernels for 0% -> 0%
where the time goes in v1:
time: 80 us; the launch traced here: 78.9 us
  Pallas kernels  72.8 us (91%)
  local copies, waits for them, and re-layouts  5.43 us (7%)
    pallas_call x1, Pallas kernels, on_device_fused(): pl.pallas_call(fused_kernel, out_shape=jax.ShapeDtypeStruct((SEQ_DEV, vis...  72.8 us

profile of v1, /device:TPU:0, one launch (start us, length us, event | category | flops | bytes accessed | tf_op | source)
XLA Modules:
  0.0 78.9 jit_solution(15318945415704583931)
XLA Ops:
  0.7 1.3 %broadcast_in_dim.15.gain1 = f32[1,1280]{1,0:T(1,128)} reshape(f32[1280]{0:T(1024)} %param.14) | data formatting | bytes 10240 | tf_op jit(solution)/shard_map/broadcast_in_dim | solution.py:412
  1.9 1.3 %broadcast_in_dim.16.gain2 = f32[1,1280]{1,0:T(1,128)} reshape(f32[1280]{0:T(1024)} %param.17) | data formatting | bytes 10240 | tf_op jit(solution)/shard_map/broadcast_in_dim | solution.py:412
  3.2 1.3 %broadcast_in_dim.17.gain_v = f32[1,1280]{1,0:T(1,128)} reshape(f32[1280]{0:T(1024)} %param.20) | data formatting | bytes 10240 | tf_op jit(solution)/shard_map/broadcast_in_dim | solution.py:413
  4.5 72.8 %shard_map.118 = bf16[96,448]{1,0:T(8,128)(2,1)} custom-call(bf16[128,128]{1,0:T(8,128)(2,1)} %fb.1, bf16[384,1280]{1,0:T(8,128)(2,1)} %conv.1, f32[1,1280]{1,0:T(1,128)} %broadcast_in_dim.15.gain1, bf16[160,1280]{1,0:T(8,128)(2,1)} %up.1, bf16[160,1280]{1,0:T(8,128)(2,1)} %bitcast.8, f32[1,1280]{1,0:T(1,128)} %broadcast_in_dim.16.gain2, ...), custom_call_target="tpu_custom_call" | custom-call | tf_op jit(solution)/shard_map/pallas_call | solution.py:402
  77.3 1.5 %copy.15 = bf16[1,96,448]{2,1,0:T(8,128)(2,1)} copy(bf16[1,96,448]{2,1,0:T(8,128)(2,1)} %bitcast.9) | data formatting | bytes 172032

commit v2 on v1

--- a/solution.py
+++ b/solution.py
@@ -161,13 +161,14 @@
     return 0.5 * x * (1.0 + lax.erf(x * 0.7071067811865476))
 
 
-FB, META, WGT, MRG, VIS, TOT, FWD, NRM, COR, XAX = 0, 7, 14, 21, 28, 35, 42, 45, 48, 49
-N_SEM = 50
+FB, META, UPW, DNW, MRG, VIS, TOT, FWD, NRM, HID, COR, XAX = 0, 7, 14, 21, 28, 35, 42, 56, 59, 62, 66, 68
+N_SEM = 70
+HALF = 640
 
 
 def fused_kernel(
     fb, conv, gain1, up, dn, gain2, aud_w, pat, gain_v, vis_w, ret, kept, out,
-    fbp, meta_s, meta, w_s, w_r, m_s, x_r, v_s, v_r, stem, hid, pa, own,
+    fbp, meta, w_s, w_r, m_s, x_r, v_s, v_r, stem, hid, pa, own,
     a_s, a_r, b_s, b_r, c_s, c_r, nrm, send_sem, recv_sem,
 ):
     me = lax.axis_index("tm")
@@ -184,12 +185,15 @@
     for peer in mod_peers:
         pl.semaphore_signal(barrier, inc=1, device_id={"mod": peer}, device_id_type=MESH)
 
+    sent = []
+
     def copy(src, dst, slot, to):
         c = pltpu.make_async_remote_copy(
             src_ref=src, dst_ref=dst, send_sem=send_sem.at[slot], recv_sem=recv_sem.at[slot],
             device_id=to, device_id_type=MESH,
         )
         c.start()
+        sent.append(c)
         return c
 
     def to_tm(src_of, dst, base):
@@ -203,22 +207,31 @@
     fbp[1040:1056] = jnp.zeros((16, 128), BF16)
     my_rows = pl.ds(pl.multiple_of(16 + me * 128, 16), 128)
     fbp[my_rows, :] = fb[...]
-    hit = ret[...] == iota((64, 64), 0)
-    inv = jnp.sum(jnp.where(hit, iota((64, 64), 1).astype(F32), 0.0), axis=1, keepdims=True)
-    kept_f = kept[...].astype(F32)
+    hit = onehot(ret[...] == iota((128, 64), 0) % 64)
+    inv = mm_nt(iota((8, 64), 1).astype(F32).astype(BF16), hit)
+    kept_f = jnp.full((8, 128), kept[0], I32).astype(F32)
     inv = jnp.where(inv < kept_f, inv, -4096.0)
-    meta_s[0:64] = jnp.broadcast_to(inv, (64, 128))
-    meta_s[64:72] = jnp.broadcast_to(kept_f, (8, 128))
-    meta[me] = meta_s[...]
+    meta[me] = jnp.where(iota((8, 128), 0) == 0, inv, kept_f)
 
     pl.semaphore_wait(barrier, TM + MOD - 2)
     fb_copies = to_tm(lambda p: fb, fbp.at[my_rows], FB)
-    meta_copies = to_tm(lambda p: meta_s, meta.at[me], META)
+    meta_copies = to_tm(lambda p: meta.at[me], meta.at[me], META)
+
+    pv = pat[pl.ds(pl.multiple_of(mo * 64, 64), 64), :].astype(F32)
+    ms = jnp.sum(pv * pv, axis=1, keepdims=True) * (1.0 / 1280.0)
+    pn = (pv * lax.rsqrt(ms + 1e-06) * gain_v[...][None, :]).astype(BF16)
+    r64, c64 = iota((64, 64), 0), iota((64, 64), 1)
+    pn = mm(onehot(c64 == 4 * (r64 % 16) + r64 // 16), pn).astype(BF16)
+    for t in range(TM):
+        q, h = t // 2, t % 2
+        m_s[t] = pn[16 * q : 16 * q + 16, HALF * h : HALF * h + HALF]
+    m_copies = to_tm(lambda p: m_s.at[p], x_r.at[me, mo], MRG)
+    x_r[me, mo] = m_s[me]
 
     row, col = iota((512, 128), 0), iota((512, 128), 1)
     for t in range(TM):
         w_s[t, 0:160] = up[:, 128 * t : 128 * t + 128]
-        w_s[t, 160:320] = dn[:, 128 * t : 128 * t + 128]
+        w_s[t, 240:400] = dn[:, 128 * t : 128 * t + 128]
     for g in range(2):
         lanes = slice(1024 + 128 * g, 1152 + 128 * g)
         rest = jnp.concatenate(
@@ -226,25 +239,16 @@
         )
         for a in range(4):
             pick = onehot((row // 128 == col // 32) & (row % 128 == 32 * a + col % 32))
-            w_s[4 * g + a, 320:400] = mm(rest, pick).astype(BF16)
-    w_copies = to_tm(lambda p: w_s.at[p], w_r.at[me], WGT)
+            w_s[4 * g + a, 160:240] = mm(rest, pick).astype(BF16)
+    up_rows, dn_rows = pl.ds(0, 240), pl.ds(240, 160)
+    u_copies = to_tm(lambda p: w_s.at[p, up_rows], w_r.at[me, up_rows], UPW)
+    d_copies = to_tm(lambda p: w_s.at[p, dn_rows], w_r.at[me, dn_rows], DNW)
     w_r[me] = w_s[me]
 
-    pv = pat[pl.ds(pl.multiple_of(mo * 64, 64), 64), :].astype(F32)
-    ms = jnp.sum(pv * pv, axis=1, keepdims=True) * (1.0 / 1280.0)
-    pn = (pv * lax.rsqrt(ms + 1e-06) * gain_v[...]).astype(BF16)
-    r64, c64 = iota((64, 64), 0), iota((64, 64), 1)
-    pn = mm(onehot(c64 == 4 * (r64 % 16) + r64 // 16), pn).astype(BF16)
-    for t in range(TM):
-        q, h = t // 2, t % 2
-        m_s[t] = pn[16 * q : 16 * q + 16, 640 * h : 640 * h + 640]
-    m_copies = to_tm(lambda p: m_s.at[p], x_r.at[mo, me], MRG)
-    x_r[mo, me] = m_s[me]
-
     arrive(fb_copies)
 
-    def stem_step(s, carry):
-        base = pl.multiple_of(s * 128, 128)
+    def stem_step(first):
+        base = pl.multiple_of(first * 128, 128)
         rows = fbp[pl.ds(base, 160), :].astype(F32)
         taps = jnp.concatenate([rows[15:143], rows[16:144], rows[17:145]], axis=1).astype(BF16)
         st = gelu(mm(taps, conv[...])).astype(BF16)
@@ -252,25 +256,47 @@
         v = st.astype(F32)
         v = v - jnp.sum(v, axis=1, keepdims=True) * (1.0 / 1280.0)
         var = jnp.sum(v * v, axis=1, keepdims=True) * (1.0 / 1280.0)
-        hid[pl.ds(base, 128), :] = (v * lax.rsqrt(var + 1e-05) * gain1[...]).astype(BF16)
-        return carry
-
-    lax.fori_loop(0, 4, stem_step, 0)
-    arrive(m_copies)
-    x_copies = [
-        copy(x_r.at[mo], x_r.at[mo], FWD + d, {"mod": p}) for d, p in enumerate(mod_peers)
-    ]
-    lax.fori_loop(4, 8, stem_step, 0)
+        hid[pl.ds(base, 128), :] = (v * lax.rsqrt(var + 1e-05) * gain1[...][None, :]).astype(BF16)
+
+    h_copies = []
+    for k in range(4):
+        x_at = 1 - xx if k < 2 else xx
+        span = 2 * (2 * x_at + cc) + k % 2
+        stem_step(span)
+        rows = pl.ds(pl.multiple_of(span * 128, 128), 128)
+        h_copies.append(copy(hid.at[rows], hid.at[rows], HID + k, {"mod": core_peer}))
+        if k == 1:
+            arrive(m_copies)
+            x_copies = [
+                copy(x_r.at[:, mo], x_r.at[:, mo], FWD + d, {"mod": p})
+                for d, p in enumerate(mod_peers)
+            ]
 
     arrive(meta_copies)
     ends, before, running = [], [], jnp.zeros((1, 128), F32)
     for s in range(TM):
         before.append(running)
-        running = running + meta[s, 64:65, :]
+        running = running + meta[s, 1:2, :]
         ends.append(running.astype(I32))
 
-    arrive(w_copies)
-    rem = jnp.concatenate([w_r[t, 320:400] for t in range(TM)], axis=0)
+    def ends_of(pair):
+        picked = []
+        for h in range(2):
+            e = ends[h]
+            for p in range(1, MOD):
+                e = jnp.where(pair == p, ends[2 * p + h], e)
+            picked.append(e)
+        return picked
+
+    def pool_rows(holder, r_s2, r_q, frames, span_ends):
+        blocks = []
+        for h in range(2):
+            j = 8 * r_q + ((holder - span_ends[h]) & 7)
+            blocks.append(onehot((r_s2 == h) & (frames // 2 == j), 0.5))
+        return jnp.concatenate(blocks, axis=1)
+
+    arrive(u_copies)
+    rem = jnp.concatenate([w_r[t, 160:240] for t in range(TM)], axis=0)
     ri, ci = iota((128, 512), 0), iota((128, 512), 1)
     rem = mm(rem, onehot((ci % 128 < 32) & (ri == 32 * (ci // 128) + ci % 128))).astype(BF16)
 
@@ -283,57 +309,52 @@
         return jnp.concatenate([main, jnp.concatenate(parts, axis=0)], axis=1)
 
     up_all = assemble(0, 0)
-    dn_all = assemble(160, 256)
-
-    def pool_rows(holder, r_s2, r_q, frames, span_ends):
-        blocks = []
-        for h in range(2):
-            j = 8 * r_q + ((holder - span_ends[h]) & 7)
-            blocks.append(onehot((r_s2 == h) & (frames // 2 == j), 0.5))
-        return jnp.concatenate(blocks, axis=1)
-
     r128, c128 = iota((128, 128), 0), iota((128, 128), 1)
-    for p in range(MOD):
-        act = gelu(mm(hid[256 * p : 256 * p + 256], up_all)).astype(BF16)
-        pool = pool_rows(r128 // 16, (r128 // 8) % 2, r128 % 8, c128, ends[2 * p : 2 * p + 2])
-        pa[p % 2, p // 2] = mm(pool, act).astype(BF16)
-
-    a_s[...] = mm_nt(pa[1 - cc].reshape(256, 256), dn_all).astype(BF16).reshape(2, 128, 1280)
-    a_copy = copy(a_s, a_r, COR, {"mod": core_peer})
-    own[...] = mm_nt(pa[cc].reshape(256, 256), dn_all).reshape(2, 128, 1280)
-    a_copy.wait_recv()
-    b_s[...] = (own[1 - xx] + a_r[1 - xx].astype(F32)).astype(BF16)
-    b_copy = copy(b_s, b_r, XAX, {"mod": x_peer})
+    order = [(1 - cc, 1 - xx), (1 - cc, xx), (cc, 1 - xx), (cc, xx)]
+    for k in (2, 0, 3, 1):
+        if k < 2:
+            arrive(h_copies[2 * k : 2 * k + 2])
+        pair = 2 * order[k][1] + order[k][0]
+        rows = pl.ds(pl.multiple_of(pair * 256, 256), 256)
+        act = gelu(mm(hid[rows, :], up_all)).astype(BF16)
+        pool = pool_rows(r128 // 16, (r128 // 8) % 2, r128 % 8, c128, ends_of(pair))
+        pa[k] = mm(pool, act).astype(BF16)
 
     arrive(x_copies)
+    lane = iota((1, 128), 1)
     pos = jnp.concatenate(
-        [meta[t, 16 * m : 16 * m + 16, :] + before[t] for m in range(MOD) for t in range(TM)], axis=0
-    )
-    pos = jnp.concatenate([pos, pos], axis=1).astype(I32)
-    lane = iota((512, 256), 1)
-    pick = onehot(pos == 8 * (lane % 32) + lane // 32)
-    chosen = mm_tn(pick, x_r[...].reshape(512, 640)).astype(BF16)
+        [
+            jnp.where(lane < 64, meta[t, 0:1, :] + before[t], meta[t + 1, 0:1, :] + before[t + 1])
+            for t in range(0, TM, 2)
+        ],
+        axis=1,
+    ).astype(I32)
+    r256 = iota((256, 512), 0)
+    pick = onehot(pos == 8 * (r256 % 32) + r256 // 32)
+    chosen = mm(pick, x_r[...].reshape(512, HALF)).astype(BF16)
     v_s[...] = mm_nt(chosen, vis_w[...]).astype(BF16).reshape(TM, 32, 448)
-
-    b_copy.wait_recv()
-    total = own[xx] + a_r[xx].astype(F32) + b_r[...].astype(F32)
-    c_s[...] = total.astype(BF16).reshape(TM, 16, 1280)
-    c_copies = to_tm(lambda p: c_s.at[p], c_r.at[me], TOT)
     v_copies = to_tm(lambda p: v_s.at[p], v_r.at[me], VIS)
-    c_r[me] = c_s[me]
     v_r[me] = v_s[me]
 
+    arrive(d_copies)
+    dn_all = assemble(240, 256)
+    a_copies = []
+    for k in range(2):
+        a_s[k] = mm_nt(pa[k], dn_all).astype(BF16)
+        a_copies.append(copy(a_s.at[k], a_r.at[k], COR + k, {"mod": core_peer}))
+    own[0] = mm_nt(pa[2], dn_all)
+    a_copies[0].wait_recv()
+    b_copies = []
+    for h in range(2):
+        cols = slice(HALF * h, HALF * h + HALF)
+        b_s[h] = (own[0, :, cols] + a_r[0, :, cols].astype(F32)).astype(BF16)
+        b_copies.append(copy(b_s.at[h], b_r.at[h], XAX + h, {"mod": x_peer}))
+    own[1] = mm_nt(pa[3], dn_all)
+    a_copies[1].wait_recv()
+
     r16, c16 = iota((16, 128), 0), iota((16, 128), 1)
-    mine = []
-    for h in range(2):
-        e = jnp.zeros((1, 128), I32)
-        for p in range(MOD):
-            e = jnp.where(mo == p, ends[2 * p + h], e)
-        mine.append(e)
-    pool = pool_rows(me, r16 // 8, r16 % 8, c16, mine)
+    pool = pool_rows(me, r16 // 8, r16 % 8, c16, ends_of(mo))
     pooled = mm(pool, stem[pl.ds(pl.multiple_of(mo * 256, 256), 256), :])
-
-    lane = iota((1, 128), 1)
     g = 8 * lane + me
     v_slot = lane
     a_slot = jnp.zeros((1, 128), I32)
@@ -344,18 +365,32 @@
     slot = jnp.where(lane < 32, v_slot, jnp.where(lane < 96, a_slot, -1))
     place = onehot(slot == iota((96, 128), 0))
 
-    arrive(c_copies)
-    for t in range(TM):
-        pooled = pooled + c_r[t].astype(F32)
-    v = pooled - jnp.sum(pooled, axis=1, keepdims=True) * (1.0 / 1280.0)
-    var = jnp.sum(v * v, axis=1, keepdims=True) * (1.0 / 1280.0)
-    nrm[mo] = (v * lax.rsqrt(var + 1e-05) * gain2[...]).astype(BF16)
-    n_copies = [copy(nrm.at[mo], nrm.at[mo], NRM + d, {"mod": p}) for d, p in enumerate(mod_peers)]
+    c_copies = []
+    for h in range(2):
+        cols = slice(HALF * h, HALF * h + HALF)
+        b_copies[h].wait_recv()
+        total = own[1, :, cols] + a_r[1, :, cols].astype(F32) + b_r[h].astype(F32)
+        c_s[h] = total.astype(BF16).reshape(TM, 16, HALF)
+        c_copies.append(to_tm(lambda p: c_s.at[h, p], c_r.at[h, me], TOT + 7 * h))
+        c_r[h, me] = c_s[h, me]
 
     arrive(v_copies)
     visual = v_r[0].astype(F32)
     for t in range(1, TM):
         visual = visual + v_r[t].astype(F32)
+
+    halves = []
+    for h in range(2):
+        arrive(c_copies[h])
+        part = pooled[:, HALF * h : HALF * h + HALF]
+        for t in range(TM):
+            part = part + c_r[h, t].astype(F32)
+        halves.append(part)
+    pooled = jnp.concatenate(halves, axis=1)
+    v = pooled - jnp.sum(pooled, axis=1, keepdims=True) * (1.0 / 1280.0)
+    var = jnp.sum(v * v, axis=1, keepdims=True) * (1.0 / 1280.0)
+    nrm[mo] = (v * lax.rsqrt(var + 1e-05) * gain2[...][None, :]).astype(BF16)
+    n_copies = [copy(nrm.at[mo], nrm.at[mo], NRM + d, {"mod": p}) for d, p in enumerate(mod_peers)]
     arrive(n_copies)
     audio = mm_nt(nrm[...].reshape(64, 1280), aud_w[...])
     tokens = jnp.concatenate(
@@ -363,11 +398,8 @@
     )
     out[...] = mm(place, tokens).astype(BF16)
 
-    for group in (fb_copies, meta_copies, w_copies, m_copies, x_copies, v_copies, c_copies, n_copies):
-        for c in group:
-            c.wait_send()
-    a_copy.wait_send()
-    b_copy.wait_send()
+    for c in sent:
+        c.wait_send()
 
 
 def on_device_fused(
@@ -377,24 +409,23 @@
     vm = pl.BlockSpec(memory_space=pltpu.VMEM)
     scratch = [
         pltpu.VMEM((1056, 128), BF16),
-        pltpu.VMEM((72, 128), F32),
-        pltpu.VMEM((TM, 72, 128), F32),
+        pltpu.VMEM((TM, 8, 128), F32),
         pltpu.VMEM((TM, 400, 128), BF16),
         pltpu.VMEM((TM, 400, 128), BF16),
-        pltpu.VMEM((TM, 16, 640), BF16),
-        pltpu.VMEM((MOD, TM, 16, 640), BF16),
+        pltpu.VMEM((TM, 16, HALF), BF16),
+        pltpu.VMEM((TM, MOD, 16, HALF), BF16),
         pltpu.VMEM((TM, 32, 448), BF16),
         pltpu.VMEM((TM, 32, 448), BF16),
         pltpu.VMEM((1024, 1280), BF16),
         pltpu.VMEM((1024, 1280), BF16),
-        pltpu.VMEM((2, 2, 128, 256), BF16),
+        pltpu.VMEM((MOD, 128, 256), BF16),
         pltpu.VMEM((2, 128, 1280), F32),
         pltpu.VMEM((2, 128, 1280), BF16),
         pltpu.VMEM((2, 128, 1280), BF16),
-        pltpu.VMEM((128, 1280), BF16),
-        pltpu.VMEM((128, 1280), BF16),
-        pltpu.VMEM((TM, 16, 1280), BF16),
-        pltpu.VMEM((TM, 16, 1280), BF16),
+        pltpu.VMEM((2, 128, HALF), BF16),
+        pltpu.VMEM((2, 128, HALF), BF16),
+        pltpu.VMEM((2, TM, 16, HALF), BF16),
+        pltpu.VMEM((2, TM, 16, HALF), BF16),
         pltpu.VMEM((MOD, 16, 1280), BF16),
         pltpu.SemaphoreType.DMA((N_SEM,)),
         pltpu.SemaphoreType.DMA((N_SEM,)),
@@ -402,15 +433,15 @@
     sequence = pl.pallas_call(
         fused_kernel,
         out_shape=jax.ShapeDtypeStruct((SEQ_DEV, vision_weight.shape[1]), BF16),
-        in_specs=[vm] * 12,
+        in_specs=[vm] * 11 + [pl.BlockSpec(memory_space=pltpu.SMEM)],
         out_specs=vm,
         scratch_shapes=scratch,
         compiler_params=pltpu.CompilerParams(
             collective_id=0, has_side_effects=True, vmem_limit_bytes=56 * 1024 * 1024
         ),
     )(
-        filterbank, conv_weight, mlp_gain[None], up_weight, down_weight.T, post_gain[None],
-        audio_weight.T, patches, vision_gain[None], vision_weight.T, retention, kept_count[None],
+        filterbank, conv_weight, mlp_gain, up_weight, down_weight.T, post_gain,
+        audio_weight.T, patches, vision_gain, vision_weight.T, retention, kept_count,
     )
     return sequence[None]
 

time: 80 us -> 64 us (0.80); the launches traced: 78.9 us -> 63.8 us
  Pallas kernels: 72.8 us -> 61.6 us
  local copies, waits for them, and re-layouts: 5.43 us -> 1.54 us
    pallas_call x1, Pallas kernels: 72.8 us -> 61.6 us  [on_device_fused(): pl.pallas_call(fused_kernel, out_shape=jax.ShapeDtypeStruct((SEQ_DEV, vis...]
    broadcast_in_dim x3 -> x0, local copies, waits for them, and re-layouts: 3.89 us -> none  [the longest x1 1.3 us: on_device_fused(): vision_gain[None]]
where the time goes in v2:
time: 64 us; the launch traced here: 63.8 us
  Pallas kernels  61.6 us (96%)
  local copies, waits for them, and re-layouts  1.54 us (2%)
  between operations  0.66 us (1%)
    pallas_call x1, Pallas kernels, on_device_fused(): pl.pallas_call(fused_kernel, out_shape=jax.ShapeDtypeStruct((SEQ_DEV, vis...  61.6 us
    unnamed x1, local copies, waits for them, and re-layouts  1.54 us

profile of v2, /device:TPU:0, one launch (start us, length us, event | category | flops | bytes accessed | tf_op | source)
XLA Modules:
  0.0 63.8 jit_solution(11065967513116555264)
XLA Ops:
  0.7 61.6 %shard_map.118 = bf16[96,448]{1,0:T(8,128)(2,1)} custom-call(bf16[128,128]{1,0:T(8,128)(2,1)} %fb.1, bf16[384,1280]{1,0:T(8,128)(2,1)} %conv.1, f32[1280]{0:T(1024)} %gain1.1, bf16[160,1280]{1,0:T(8,128)(2,1)} %up.1, bf16[160,1280]{1,0:T(8,128)(2,1)} %bitcast.6, f32[1280]{0:T(1024)} %gain2.1, bf16[448,1280]{1,0:T(8,128)(2,1)} %bitcast.4, ...), custom_call_target="tpu_custom_call" | custom-call | tf_op jit(solution)/shard_map/pallas_call | solution.py:433
  62.3 1.5 %copy.15 = bf16[1,96,448]{2,1,0:T(8,128)(2,1)} copy(bf16[1,96,448]{2,1,0:T(8,128)(2,1)} %bitcast.7) | data formatting | bytes 172032

commit v3 on v2

--- a/solution.py
+++ b/solution.py
@@ -161,29 +161,46 @@
     return 0.5 * x * (1.0 + lax.erf(x * 0.7071067811865476))
 
 
-FB, META, UPW, DNW, MRG, VIS, TOT, FWD, NRM, HID, COR, XAX = 0, 7, 14, 21, 28, 35, 42, 56, 59, 62, 66, 68
-N_SEM = 70
+FB, META, UPW, DNW, MRG, VIS, TOT, UPX, DNX, FWD, NRM, HID, COR = 0, 7, 14, 21, 28, 35, 42, 56, 64, 72, 75, 78, 80
+N_SEM = 82
 HALF = 640
+FLIPS = (4, 6, 5, 7, 2, 3, 1)
+
+
+def flipped(index, bits):
+    for bit in (1, 2, 4):
+        if bits % (2 * bit) >= bit:
+            index = index + bit - 2 * bit * ((index // bit) % 2)
+    return index
 
 
 def fused_kernel(
-    fb, conv, gain1, up, dn, gain2, aud_w, pat, gain_v, vis_w, ret, kept, out,
-    fbp, meta, w_s, w_r, m_s, x_r, v_s, v_r, stem, hid, pa, own,
-    a_s, a_r, b_s, b_r, c_s, c_r, nrm, send_sem, recv_sem,
+    fb, conv_h, gain1, up, dn, gain2, aud_h, pat_h, gain_v, vis_h, ret, kept, out,
+    conv, aud_w, pat, vis_w, fbp, meta, w_s, w_r, m_s, x_r, v_s, v_r, stem, hid, pa,
+    a_s, a_r, c_s, c_r, nrm, load_sem, send_sem, recv_sem,
 ):
     me = lax.axis_index("tm")
     mo = lax.axis_index("mod")
     xx, cc = mo // 2, mo % 2
-    tm_peers = [lax.rem(me + d, TM) for d in range(1, TM)]
-    mod_peers = [lax.rem(mo + d, MOD) for d in range(1, MOD)]
-    core_peer = xx * 2 + (1 - cc)
-    x_peer = (1 - xx) * 2 + cc
+    tm_peers = [flipped(me, bits) for bits in FLIPS]
+    mod_peers = [flipped(mo, bits) for bits in (2, 3, 1)]
+    x_peer, core_peer = mod_peers[0], mod_peers[2]
 
     barrier = pltpu.get_barrier_semaphore()
     for peer in tm_peers:
         pl.semaphore_signal(barrier, inc=1, device_id={"tm": peer}, device_id_type=MESH)
     for peer in mod_peers:
         pl.semaphore_signal(barrier, inc=1, device_id={"mod": peer}, device_id_type=MESH)
+
+    quarter = pl.ds(pl.multiple_of(mo * 64, 64), 64)
+    loads = [
+        pltpu.make_async_copy(src, dst, load_sem.at[i])
+        for i, (src, dst) in enumerate(
+            [(pat_h.at[quarter], pat), (conv_h, conv), (vis_h, vis_w), (aud_h, aud_w)]
+        )
+    ]
+    for c in loads:
+        c.start()
 
     sent = []
 
@@ -213,20 +230,22 @@
     inv = jnp.where(inv < kept_f, inv, -4096.0)
     meta[me] = jnp.where(iota((8, 128), 0) == 0, inv, kept_f)
 
+    def needed(span):
+        return (span + 1 >= 2 * mo) & (span <= 2 * mo + 2)
+
+    fb_copies = [
+        pltpu.make_async_remote_copy(
+            src_ref=fb, dst_ref=fbp.at[my_rows], send_sem=send_sem.at[FB + d],
+            recv_sem=recv_sem.at[FB + d], device_id={"tm": p}, device_id_type=MESH,
+        )
+        for d, p in enumerate(tm_peers)
+    ]
     pl.semaphore_wait(barrier, TM + MOD - 2)
-    fb_copies = to_tm(lambda p: fb, fbp.at[my_rows], FB)
-    meta_copies = to_tm(lambda p: meta.at[me], meta.at[me], META)
-
-    pv = pat[pl.ds(pl.multiple_of(mo * 64, 64), 64), :].astype(F32)
-    ms = jnp.sum(pv * pv, axis=1, keepdims=True) * (1.0 / 1280.0)
-    pn = (pv * lax.rsqrt(ms + 1e-06) * gain_v[...][None, :]).astype(BF16)
-    r64, c64 = iota((64, 64), 0), iota((64, 64), 1)
-    pn = mm(onehot(c64 == 4 * (r64 % 16) + r64 // 16), pn).astype(BF16)
-    for t in range(TM):
-        q, h = t // 2, t % 2
-        m_s[t] = pn[16 * q : 16 * q + 16, HALF * h : HALF * h + HALF]
-    m_copies = to_tm(lambda p: m_s.at[p], x_r.at[me, mo], MRG)
-    x_r[me, mo] = m_s[me]
+
+    @pl.when(needed(me))
+    def _():
+        for c in fb_copies:
+            c.start()
 
     row, col = iota((512, 128), 0), iota((512, 128), 1)
     for t in range(TM):
@@ -240,37 +259,55 @@
         for a in range(4):
             pick = onehot((row // 128 == col // 32) & (row % 128 == 32 * a + col % 32))
             w_s[4 * g + a, 160:240] = mm(rest, pick).astype(BF16)
+    w_r[0, me] = w_s[me]
     up_rows, dn_rows = pl.ds(0, 240), pl.ds(240, 160)
-    u_copies = to_tm(lambda p: w_s.at[p, up_rows], w_r.at[me, up_rows], UPW)
-    d_copies = to_tm(lambda p: w_s.at[p, dn_rows], w_r.at[me, dn_rows], DNW)
-    w_r[me] = w_s[me]
-
-    arrive(fb_copies)
-
-    def stem_step(first):
-        base = pl.multiple_of(first * 128, 128)
+    u_copies = to_tm(lambda p: w_s.at[p, up_rows], w_r.at[0, me, up_rows], UPW)
+
+    def to_x(source, rows, slot):
+        return copy(w_r.at[0, source, rows], w_r.at[1, source, rows], slot, {"mod": x_peer})
+
+    ux_copies = [to_x(me, up_rows, UPX + 7)]
+    dx_copies = [to_x(me, dn_rows, DNX + 7)]
+    meta_copies = to_tm(lambda p: meta.at[me], meta.at[me], META)
+
+    loads[0].wait()
+    pv = pat[...].astype(F32)
+    ms = jnp.sum(pv * pv, axis=1, keepdims=True) * (1.0 / 1280.0)
+    pn = (pv * lax.rsqrt(ms + 1e-06) * gain_v[...][None, :]).astype(BF16)
+    r64, c64 = iota((64, 64), 0), iota((64, 64), 1)
+    pn = mm(onehot(c64 == 4 * (r64 % 16) + r64 // 16), pn).astype(BF16)
+    for t in range(TM):
+        q, h = t // 2, t % 2
+        m_s[t] = pn[16 * q : 16 * q + 16, HALF * h : HALF * h + HALF]
+    m_copies = to_tm(lambda p: m_s.at[p], x_r.at[me, mo], MRG)
+    x_r[me, mo] = m_s[me]
+    d_copies = to_tm(lambda p: w_s.at[p, dn_rows], w_r.at[0, me, dn_rows], DNW)
+
+    loads[1].wait()
+    for c, p in zip(fb_copies, tm_peers):
+        pl.when(needed(p))(c.wait_recv)
+    h_copies = []
+    for k in range(2):
+        base = pl.multiple_of((2 * mo + k) * 128, 128)
         rows = fbp[pl.ds(base, 160), :].astype(F32)
         taps = jnp.concatenate([rows[15:143], rows[16:144], rows[17:145]], axis=1).astype(BF16)
         st = gelu(mm(taps, conv[...])).astype(BF16)
-        stem[pl.ds(base, 128), :] = st
+        stem[128 * k : 128 * k + 128] = st
         v = st.astype(F32)
         v = v - jnp.sum(v, axis=1, keepdims=True) * (1.0 / 1280.0)
         var = jnp.sum(v * v, axis=1, keepdims=True) * (1.0 / 1280.0)
-        hid[pl.ds(base, 128), :] = (v * lax.rsqrt(var + 1e-05) * gain1[...][None, :]).astype(BF16)
-
-    h_copies = []
-    for k in range(4):
-        x_at = 1 - xx if k < 2 else xx
-        span = 2 * (2 * x_at + cc) + k % 2
-        stem_step(span)
-        rows = pl.ds(pl.multiple_of(span * 128, 128), 128)
-        h_copies.append(copy(hid.at[rows], hid.at[rows], HID + k, {"mod": core_peer}))
-        if k == 1:
-            arrive(m_copies)
-            x_copies = [
-                copy(x_r.at[:, mo], x_r.at[:, mo], FWD + d, {"mod": p})
-                for d, p in enumerate(mod_peers)
-            ]
+        part = pl.ds(128 * k, 128)
+        hid[cc, part] = (v * lax.rsqrt(var + 1e-05) * gain1[...][None, :]).astype(BF16)
+        h_copies.append(copy(hid.at[cc, part], hid.at[cc, part], HID + k, {"mod": core_peer}))
+
+    for d in range(7):
+        u_copies[d].wait_recv()
+        ux_copies.append(to_x(tm_peers[d], up_rows, UPX + d))
+    arrive(m_copies)
+    x_copies = [
+        copy(x_r.at[:, mo], x_r.at[:, mo], FWD, {"mod": x_peer}),
+        copy(x_r.at[:, mo], x_r.at[:, mo], FWD + 1, {"mod": core_peer}),
+    ]
 
     arrive(meta_copies)
     ends, before, running = [], [], jnp.zeros((1, 128), F32)
@@ -295,32 +332,49 @@
             blocks.append(onehot((r_s2 == h) & (frames // 2 == j), 0.5))
         return jnp.concatenate(blocks, axis=1)
 
-    arrive(u_copies)
-    rem = jnp.concatenate([w_r[t, 160:240] for t in range(TM)], axis=0)
-    ri, ci = iota((128, 512), 0), iota((128, 512), 1)
-    rem = mm(rem, onehot((ci % 128 < 32) & (ri == 32 * (ci // 128) + ci % 128))).astype(BF16)
+    arrive(ux_copies)
+    rem = jnp.concatenate(
+        [jnp.concatenate([w_r[i, t, 160:240] for t in range(TM)], axis=0) for i in range(2)], axis=1
+    )
+    ri, ci = iota((256, 512), 0), iota((256, 512), 1)
+    unit = ci % 128
+    pick = onehot((unit < 64) & (ri == 128 * (unit // 32) + 32 * (ci // 128) + unit % 32))
+    rem = mm(rem, pick).astype(BF16)
 
     def assemble(first, lane):
-        main = jnp.concatenate([w_r[t, first : first + 160] for t in range(TM)], axis=0)
         parts = []
         for t in range(TM):
             parts.append(rem[80 * t : 80 * t + 80, lane : lane + 128])
             parts.append(rem[80 * t : 80 * t + 80, lane + 128 : lane + 256])
-        return jnp.concatenate([main, jnp.concatenate(parts, axis=0)], axis=1)
+        mains = [
+            jnp.concatenate([w_r[i, t, first : first + 160] for t in range(TM)], axis=0)
+            for i in range(2)
+        ]
+        return jnp.concatenate(mains + [jnp.concatenate(parts, axis=0)], axis=1)
 
     up_all = assemble(0, 0)
     r128, c128 = iota((128, 128), 0), iota((128, 128), 1)
-    order = [(1 - cc, 1 - xx), (1 - cc, xx), (cc, 1 - xx), (cc, xx)]
-    for k in (2, 0, 3, 1):
-        if k < 2:
-            arrive(h_copies[2 * k : 2 * k + 2])
-        pair = 2 * order[k][1] + order[k][0]
-        rows = pl.ds(pl.multiple_of(pair * 256, 256), 256)
-        act = gelu(mm(hid[rows, :], up_all)).astype(BF16)
-        pool = pool_rows(r128 // 16, (r128 // 8) % 2, r128 % 8, c128, ends_of(pair))
+
+    def feed(k, core):
+        act = gelu(mm(hid[core], up_all)).astype(BF16)
+        pool = pool_rows(r128 // 16, (r128 // 8) % 2, r128 % 8, c128, ends_of(2 * xx + core))
         pa[k] = mm(pool, act).astype(BF16)
 
-    arrive(x_copies)
+    def forward_down(steps):
+        for d in steps:
+            d_copies[d].wait_recv()
+            dx_copies.append(to_x(tm_peers[d], dn_rows, DNX + d))
+
+    feed(0, cc)
+    x_copies[0].wait_recv()
+    x_copies.append(copy(x_r.at[:, x_peer], x_r.at[:, x_peer], FWD + 2, {"mod": core_peer}))
+    forward_down(range(0, 4))
+    arrive(h_copies)
+    feed(1, 1 - cc)
+    forward_down(range(4, 7))
+
+    arrive(x_copies[1:])
+    loads[2].wait()
     lane = iota((1, 128), 1)
     pos = jnp.concatenate(
         [
@@ -336,25 +390,22 @@
     v_copies = to_tm(lambda p: v_s.at[p], v_r.at[me], VIS)
     v_r[me] = v_s[me]
 
-    arrive(d_copies)
+    arrive(dx_copies)
     dn_all = assemble(240, 256)
     a_copies = []
-    for k in range(2):
-        a_s[k] = mm_nt(pa[k], dn_all).astype(BF16)
-        a_copies.append(copy(a_s.at[k], a_r.at[k], COR + k, {"mod": core_peer}))
-    own[0] = mm_nt(pa[2], dn_all)
-    a_copies[0].wait_recv()
-    b_copies = []
     for h in range(2):
-        cols = slice(HALF * h, HALF * h + HALF)
-        b_s[h] = (own[0, :, cols] + a_r[0, :, cols].astype(F32)).astype(BF16)
-        b_copies.append(copy(b_s.at[h], b_r.at[h], XAX + h, {"mod": x_peer}))
-    own[1] = mm_nt(pa[3], dn_all)
-    a_copies[1].wait_recv()
+        a_s[h] = mm_nt(pa[1], dn_all[HALF * h : HALF * h + HALF]).astype(BF16)
+        a_copies.append(copy(a_s.at[h], a_r.at[h], COR + h, {"mod": core_peer}))
+    c_copies = []
+    for h in range(2):
+        own = mm_nt(pa[0], dn_all[HALF * h : HALF * h + HALF])
+        a_copies[h].wait_recv()
+        c_s[h] = (own + a_r[h].astype(F32)).astype(BF16).reshape(TM, 16, HALF)
+        c_copies.append(to_tm(lambda p: c_s.at[h, p], c_r.at[h, me], TOT + 7 * h))
+        c_r[h, me] = c_s[h, me]
 
     r16, c16 = iota((16, 128), 0), iota((16, 128), 1)
-    pool = pool_rows(me, r16 // 8, r16 % 8, c16, ends_of(mo))
-    pooled = mm(pool, stem[pl.ds(pl.multiple_of(mo * 256, 256), 256), :])
+    pooled = mm(pool_rows(me, r16 // 8, r16 % 8, c16, ends_of(mo)), stem[...])
     g = 8 * lane + me
     v_slot = lane
     a_slot = jnp.zeros((1, 128), I32)
@@ -364,15 +415,6 @@
         a_slot = jnp.where((lane - 32) // 8 == s, ((ends[s] + j) >> 3) + 8 * s, a_slot)
     slot = jnp.where(lane < 32, v_slot, jnp.where(lane < 96, a_slot, -1))
     place = onehot(slot == iota((96, 128), 0))
-
-    c_copies = []
-    for h in range(2):
-        cols = slice(HALF * h, HALF * h + HALF)
-        b_copies[h].wait_recv()
-        total = own[1, :, cols] + a_r[1, :, cols].astype(F32) + b_r[h].astype(F32)
-        c_s[h] = total.astype(BF16).reshape(TM, 16, HALF)
-        c_copies.append(to_tm(lambda p: c_s.at[h, p], c_r.at[h, me], TOT + 7 * h))
-        c_r[h, me] = c_s[h, me]
 
     arrive(v_copies)
     visual = v_r[0].astype(F32)
@@ -391,6 +433,7 @@
     var = jnp.sum(v * v, axis=1, keepdims=True) * (1.0 / 1280.0)
     nrm[mo] = (v * lax.rsqrt(var + 1e-05) * gain2[...][None, :]).astype(BF16)
     n_copies = [copy(nrm.at[mo], nrm.at[mo], NRM + d, {"mod": p}) for d, p in enumerate(mod_peers)]
+    loads[3].wait()
     arrive(n_copies)
     audio = mm_nt(nrm[...].reshape(64, 1280), aud_w[...])
     tokens = jnp.concatenate(
@@ -400,6 +443,11 @@
 
     for c in sent:
         c.wait_send()
+
+    @pl.when(needed(me))
+    def _():
+        for c in fb_copies:
+            c.wait_send()
 
 
 def on_device_fused(
@@ -407,33 +455,37 @@
     patches, vision_gain, vision_weight, retention, kept_count,
 ):
     vm = pl.BlockSpec(memory_space=pltpu.VMEM)
+    far = pl.BlockSpec(memory_space=pl.ANY)
+    n_out = vision_weight.shape[1]
     scratch = [
+        pltpu.VMEM(conv_weight.shape, BF16),
+        pltpu.VMEM((n_out, 1280), BF16),
+        pltpu.VMEM((64, 1280), BF16),
+        pltpu.VMEM((n_out, HALF), BF16),
         pltpu.VMEM((1056, 128), BF16),
         pltpu.VMEM((TM, 8, 128), F32),
         pltpu.VMEM((TM, 400, 128), BF16),
-        pltpu.VMEM((TM, 400, 128), BF16),
+        pltpu.VMEM((2, TM, 400, 128), BF16),
         pltpu.VMEM((TM, 16, HALF), BF16),
         pltpu.VMEM((TM, MOD, 16, HALF), BF16),
-        pltpu.VMEM((TM, 32, 448), BF16),
-        pltpu.VMEM((TM, 32, 448), BF16),
-        pltpu.VMEM((1024, 1280), BF16),
-        pltpu.VMEM((1024, 1280), BF16),
-        pltpu.VMEM((MOD, 128, 256), BF16),
-        pltpu.VMEM((2, 128, 1280), F32),
-        pltpu.VMEM((2, 128, 1280), BF16),
-        pltpu.VMEM((2, 128, 1280), BF16),
+        pltpu.VMEM((TM, 32, n_out), BF16),
+        pltpu.VMEM((TM, 32, n_out), BF16),
+        pltpu.VMEM((256, 1280), BF16),
+        pltpu.VMEM((2, 256, 1280), BF16),
+        pltpu.VMEM((2, 128, 384), BF16),
         pltpu.VMEM((2, 128, HALF), BF16),
         pltpu.VMEM((2, 128, HALF), BF16),
         pltpu.VMEM((2, TM, 16, HALF), BF16),
         pltpu.VMEM((2, TM, 16, HALF), BF16),
         pltpu.VMEM((MOD, 16, 1280), BF16),
+        pltpu.SemaphoreType.DMA((4,)),
         pltpu.SemaphoreType.DMA((N_SEM,)),
         pltpu.SemaphoreType.DMA((N_SEM,)),
     ]
     sequence = pl.pallas_call(
         fused_kernel,
         out_shape=jax.ShapeDtypeStruct((SEQ_DEV, vision_weight.shape[1]), BF16),
-        in_specs=[vm] * 11 + [pl.BlockSpec(memory_space=pltpu.SMEM)],
+        in_specs=[vm, far, vm, vm, vm, vm, far, far, vm, far, vm, pl.BlockSpec(memory_space=pltpu.SMEM)],
         out_specs=vm,
         scratch_shapes=scratch,
         compiler_params=pltpu.CompilerParams(

time: 64 us -> 67.1 us (1.048)
  Pallas kernels: 61.6 us -> 64.7 us
    pallas_call x1, Pallas kernels: 61.6 us -> 64.7 us  [on_device_fused(): pl.pallas_call(fused_kernel, out_shape=jax.ShapeDtypeStruct((SEQ_DEV, vis...]
where the time goes in v3:
time: 67.1 us; the launch traced here: 66.9 us
  Pallas kernels  64.7 us (96%)
  local copies, waits for them, and re-layouts  1.54 us (2%)
    pallas_call x1, Pallas kernels, on_device_fused(): pl.pallas_call(fused_kernel, out_shape=jax.ShapeDtypeStruct((SEQ_DEV, vis...  64.7 us
    unnamed x1, local copies, waits for them, and re-layouts  1.54 us

profile of v3, /device:TPU:0, one launch (start us, length us, event | category | flops | bytes accessed | tf_op | source)
XLA Modules:
  0.0 66.9 jit_solution(15704245377182097577)
XLA Ops:
  0.7 64.7 %shard_map.118 = bf16[96,448]{1,0:T(8,128)(2,1)} custom-call(bf16[128,128]{1,0:T(8,128)(2,1)} %fb.1, bf16[384,1280]{1,0:T(8,128)(2,1)} %conv_h.1, f32[1280]{0:T(1024)} %gain1.1, bf16[160,1280]{1,0:T(8,128)(2,1)} %up.1, bf16[160,1280]{1,0:T(8,128)(2,1)} %bitcast.6, f32[1280]{0:T(1024)} %gain2.1, bf16[448,1280]{1,0:T(8,128)(2,1)} %bitcast.4, ...), custom_call_target="tpu_custom_call" | custom-call | tf_op jit(solution)/shard_map/pallas_call | solution.py:485
  65.3 1.5 %copy.15 = bf16[1,96,448]{2,1,0:T(8,128)(2,1)} copy(bf16[1,96,448]{2,1,0:T(8,128)(2,1)} %bitcast.7) | data formatting | bytes 172032

commit v4 on v2

--- a/solution.py
+++ b/solution.py
@@ -164,26 +164,43 @@
 FB, META, UPW, DNW, MRG, VIS, TOT, FWD, NRM, HID, COR, XAX = 0, 7, 14, 21, 28, 35, 42, 56, 59, 62, 66, 68
 N_SEM = 70
 HALF = 640
+FLIPS = (4, 6, 5, 7, 2, 3, 1)
+
+
+def flipped(index, bits):
+    for bit in (1, 2, 4):
+        if bits % (2 * bit) >= bit:
+            index = index + bit - 2 * bit * ((index // bit) % 2)
+    return index
 
 
 def fused_kernel(
-    fb, conv, gain1, up, dn, gain2, aud_w, pat, gain_v, vis_w, ret, kept, out,
-    fbp, meta, w_s, w_r, m_s, x_r, v_s, v_r, stem, hid, pa, own,
-    a_s, a_r, b_s, b_r, c_s, c_r, nrm, send_sem, recv_sem,
+    fb, conv_h, gain1, up, dn, gain2, aud_h, pat_h, gain_v, vis_h, ret, kept, out,
+    conv, aud_w, pat, vis_w, fbp, meta, w_s, w_r, m_s, x_r, v_s, v_r, stem, hid, pa, own,
+    a_s, a_r, b_s, b_r, c_s, c_r, nrm, load_sem, send_sem, recv_sem,
 ):
     me = lax.axis_index("tm")
     mo = lax.axis_index("mod")
     xx, cc = mo // 2, mo % 2
-    tm_peers = [lax.rem(me + d, TM) for d in range(1, TM)]
-    mod_peers = [lax.rem(mo + d, MOD) for d in range(1, MOD)]
-    core_peer = xx * 2 + (1 - cc)
-    x_peer = (1 - xx) * 2 + cc
+    tm_peers = [flipped(me, bits) for bits in FLIPS]
+    mod_peers = [flipped(mo, bits) for bits in (2, 3, 1)]
+    x_peer, core_peer = mod_peers[0], mod_peers[2]
 
     barrier = pltpu.get_barrier_semaphore()
     for peer in tm_peers:
         pl.semaphore_signal(barrier, inc=1, device_id={"tm": peer}, device_id_type=MESH)
     for peer in mod_peers:
         pl.semaphore_signal(barrier, inc=1, device_id={"mod": peer}, device_id_type=MESH)
+
+    quarter = pl.ds(pl.multiple_of(mo * 64, 64), 64)
+    loads = [
+        pltpu.make_async_copy(src, dst, load_sem.at[i])
+        for i, (src, dst) in enumerate(
+            [(pat_h.at[quarter], pat), (conv_h, conv), (vis_h, vis_w), (aud_h, aud_w)]
+        )
+    ]
+    for c in loads:
+        c.start()
 
     sent = []
 
@@ -213,11 +230,48 @@
     inv = jnp.where(inv < kept_f, inv, -4096.0)
     meta[me] = jnp.where(iota((8, 128), 0) == 0, inv, kept_f)
 
+    row, col = iota((512, 128), 0), iota((512, 128), 1)
+    for t in range(TM):
+        w_s[t, 0:160] = up[:, 128 * t : 128 * t + 128]
+        w_s[t, 240:400] = dn[:, 128 * t : 128 * t + 128]
+    picks = [onehot((row // 128 == col // 32) & (row % 128 == 32 * a + col % 32)) for a in range(4)]
+    for g in range(2):
+        lanes = slice(1024 + 128 * g, 1152 + 128 * g)
+        rest = jnp.concatenate(
+            [up[0:80, lanes], up[80:160, lanes], dn[0:80, lanes], dn[80:160, lanes]], axis=1
+        )
+        for a in range(4):
+            w_s[4 * g + a, 160:240] = mm(rest, picks[a]).astype(BF16)
+    w_r[me] = w_s[me]
+
+    def frames(d, p, source):
+        first = 112 * (source % 2)
+        edge = pl.ds(pl.multiple_of(first, 16), 16)
+        there = pl.ds(pl.multiple_of(16 + source * 128 + first, 16), 16)
+        whole = pl.ds(pl.multiple_of(16 + source * 128, 16), 128)
+        return [
+            pltpu.make_async_remote_copy(
+                src_ref=src, dst_ref=dst, send_sem=send_sem.at[FB + d], recv_sem=recv_sem.at[FB + d],
+                device_id={"tm": p}, device_id_type=MESH,
+            )
+            for src, dst in ((fb, fbp.at[whole]), (fb.at[edge], fbp.at[there]))
+        ]
+
+    def both_ways(source, act):
+        here = (source // 2) % 2 == cc
+        pl.when(here)(lambda: act(0))
+        pl.when(jnp.logical_not(here))(lambda: act(1))
+
+    fb_out = [frames(d, p, me) for d, p in enumerate(tm_peers)]
+    fb_in = [frames(d, p, p) for d, p in enumerate(tm_peers)]
     pl.semaphore_wait(barrier, TM + MOD - 2)
-    fb_copies = to_tm(lambda p: fb, fbp.at[my_rows], FB)
+    both_ways(me, lambda i: [c[i].start() for c in fb_out] and None)
+    up_rows, dn_rows = pl.ds(0, 240), pl.ds(240, 160)
+    u_copies = to_tm(lambda p: w_s.at[p, up_rows], w_r.at[me, up_rows], UPW)
     meta_copies = to_tm(lambda p: meta.at[me], meta.at[me], META)
 
-    pv = pat[pl.ds(pl.multiple_of(mo * 64, 64), 64), :].astype(F32)
+    loads[0].wait()
+    pv = pat[...].astype(F32)
     ms = jnp.sum(pv * pv, axis=1, keepdims=True) * (1.0 / 1280.0)
     pn = (pv * lax.rsqrt(ms + 1e-06) * gain_v[...][None, :]).astype(BF16)
     r64, c64 = iota((64, 64), 0), iota((64, 64), 1)
@@ -227,25 +281,11 @@
         m_s[t] = pn[16 * q : 16 * q + 16, HALF * h : HALF * h + HALF]
     m_copies = to_tm(lambda p: m_s.at[p], x_r.at[me, mo], MRG)
     x_r[me, mo] = m_s[me]
-
-    row, col = iota((512, 128), 0), iota((512, 128), 1)
-    for t in range(TM):
-        w_s[t, 0:160] = up[:, 128 * t : 128 * t + 128]
-        w_s[t, 240:400] = dn[:, 128 * t : 128 * t + 128]
-    for g in range(2):
-        lanes = slice(1024 + 128 * g, 1152 + 128 * g)
-        rest = jnp.concatenate(
-            [up[0:80, lanes], up[80:160, lanes], dn[0:80, lanes], dn[80:160, lanes]], axis=1
-        )
-        for a in range(4):
-            pick = onehot((row // 128 == col // 32) & (row % 128 == 32 * a + col % 32))
-            w_s[4 * g + a, 160:240] = mm(rest, pick).astype(BF16)
-    up_rows, dn_rows = pl.ds(0, 240), pl.ds(240, 160)
-    u_copies = to_tm(lambda p: w_s.at[p, up_rows], w_r.at[me, up_rows], UPW)
     d_copies = to_tm(lambda p: w_s.at[p, dn_rows], w_r.at[me, dn_rows], DNW)
-    w_r[me] = w_s[me]
-
-    arrive(fb_copies)
+
+    loads[1].wait()
+    for d, p in enumerate(tm_peers):
+        both_ways(p, lambda i: fb_in[d][i].wait_recv())
 
     def stem_step(first):
         base = pl.multiple_of(first * 128, 128)
@@ -332,25 +372,23 @@
     r256 = iota((256, 512), 0)
     pick = onehot(pos == 8 * (r256 % 32) + r256 // 32)
     chosen = mm(pick, x_r[...].reshape(512, HALF)).astype(BF16)
+    loads[2].wait()
     v_s[...] = mm_nt(chosen, vis_w[...]).astype(BF16).reshape(TM, 32, 448)
     v_copies = to_tm(lambda p: v_s.at[p], v_r.at[me], VIS)
     v_r[me] = v_s[me]
 
     arrive(d_copies)
     dn_all = assemble(240, 256)
-    a_copies = []
-    for k in range(2):
-        a_s[k] = mm_nt(pa[k], dn_all).astype(BF16)
-        a_copies.append(copy(a_s.at[k], a_r.at[k], COR + k, {"mod": core_peer}))
-    own[0] = mm_nt(pa[2], dn_all)
-    a_copies[0].wait_recv()
-    b_copies = []
+    a_copies, b_copies, c_copies = [], [], []
     for h in range(2):
-        cols = slice(HALF * h, HALF * h + HALF)
-        b_s[h] = (own[0, :, cols] + a_r[0, :, cols].astype(F32)).astype(BF16)
+        product = mm_nt(pa[...].reshape(512, 256), dn_all[HALF * h : HALF * h + HALF])
+        a_s[h] = product[0:256].astype(BF16)
+        a_copies.append(copy(a_s.at[h], a_r.at[h], COR + h, {"mod": core_peer}))
+        own[h] = product[256:512]
+    for h in range(2):
+        a_copies[h].wait_recv()
+        b_s[h] = (own[h, 0:128] + a_r[h, 0:128].astype(F32)).astype(BF16)
         b_copies.append(copy(b_s.at[h], b_r.at[h], XAX + h, {"mod": x_peer}))
-    own[1] = mm_nt(pa[3], dn_all)
-    a_copies[1].wait_recv()
 
     r16, c16 = iota((16, 128), 0), iota((16, 128), 1)
     pool = pool_rows(me, r16 // 8, r16 % 8, c16, ends_of(mo))
@@ -365,11 +403,10 @@
     slot = jnp.where(lane < 32, v_slot, jnp.where(lane < 96, a_slot, -1))
     place = onehot(slot == iota((96, 128), 0))
 
-    c_copies = []
     for h in range(2):
-        cols = slice(HALF * h, HALF * h + HALF)
+        total = own[h, 128:256] + a_r[h, 128:256].astype(F32)
         b_copies[h].wait_recv()
-        total = own[1, :, cols] + a_r[1, :, cols].astype(F32) + b_r[h].astype(F32)
+        total = total + b_r[h].astype(F32)
         c_s[h] = total.astype(BF16).reshape(TM, 16, HALF)
         c_copies.append(to_tm(lambda p: c_s.at[h, p], c_r.at[h, me], TOT + 7 * h))
         c_r[h, me] = c_s[h, me]
@@ -391,6 +428,7 @@
     var = jnp.sum(v * v, axis=1, keepdims=True) * (1.0 / 1280.0)
     nrm[mo] = (v * lax.rsqrt(var + 1e-05) * gain2[...][None, :]).astype(BF16)
     n_copies = [copy(nrm.at[mo], nrm.at[mo], NRM + d, {"mod": p}) for d, p in enumerate(mod_peers)]
+    loads[3].wait()
     arrive(n_copies)
     audio = mm_nt(nrm[...].reshape(64, 1280), aud_w[...])
     tokens = jnp.concatenate(
@@ -400,6 +438,7 @@
 
     for c in sent:
         c.wait_send()
+    both_ways(me, lambda i: [c[i].wait_send() for c in fb_out] and None)
 
 
 def on_device_fused(
@@ -407,33 +446,40 @@
     patches, vision_gain, vision_weight, retention, kept_count,
 ):
     vm = pl.BlockSpec(memory_space=pltpu.VMEM)
+    far = pl.BlockSpec(memory_space=pl.ANY)
+    n_out = vision_weight.shape[1]
     scratch = [
+        pltpu.VMEM(conv_weight.shape, BF16),
+        pltpu.VMEM((n_out, 1280), BF16),
+        pltpu.VMEM((64, 1280), BF16),
+        pltpu.VMEM((n_out, HALF), BF16),
         pltpu.VMEM((1056, 128), BF16),
         pltpu.VMEM((TM, 8, 128), F32),
         pltpu.VMEM((TM, 400, 128), BF16),
         pltpu.VMEM((TM, 400, 128), BF16),
         pltpu.VMEM((TM, 16, HALF), BF16),
         pltpu.VMEM((TM, MOD, 16, HALF), BF16),
-        pltpu.VMEM((TM, 32, 448), BF16),
-        pltpu.VMEM((TM, 32, 448), BF16),
+        pltpu.VMEM((TM, 32, n_out), BF16),
+        pltpu.VMEM((TM, 32, n_out), BF16),
         pltpu.VMEM((1024, 1280), BF16),
         pltpu.VMEM((1024, 1280), BF16),
         pltpu.VMEM((MOD, 128, 256), BF16),
-        pltpu.VMEM((2, 128, 1280), F32),
-        pltpu.VMEM((2, 128, 1280), BF16),
-        pltpu.VMEM((2, 128, 1280), BF16),
+        pltpu.VMEM((2, 256, HALF), F32),
+        pltpu.VMEM((2, 256, HALF), BF16),
+        pltpu.VMEM((2, 256, HALF), BF16),
         pltpu.VMEM((2, 128, HALF), BF16),
         pltpu.VMEM((2, 128, HALF), BF16),
         pltpu.VMEM((2, TM, 16, HALF), BF16),
         pltpu.VMEM((2, TM, 16, HALF), BF16),
         pltpu.VMEM((MOD, 16, 1280), BF16),
+        pltpu.SemaphoreType.DMA((4,)),
         pltpu.SemaphoreType.DMA((N_SEM,)),
         pltpu.SemaphoreType.DMA((N_SEM,)),
     ]
     sequence = pl.pallas_call(
         fused_kernel,
         out_shape=jax.ShapeDtypeStruct((SEQ_DEV, vision_weight.shape[1]), BF16),
-        in_specs=[vm] * 11 + [pl.BlockSpec(memory_space=pltpu.SMEM)],
+        in_specs=[vm, far, vm, vm, vm, vm, far, far, vm, far, vm, pl.BlockSpec(memory_space=pltpu.SMEM)],
         out_specs=vm,
         scratch_shapes=scratch,
         compiler_params=pltpu.CompilerParams(

time: 64 us -> 64.7 us (1.011)
  Pallas kernels: 61.6 us -> 62.3 us
    pallas_call x1, Pallas kernels: 61.6 us -> 62.3 us  [on_device_fused(): pl.pallas_call(fused_kernel, out_shape=jax.ShapeDtypeStruct((SEQ_DEV, vis...]
where the time goes in v4:
time: 64.7 us; the launch traced here: 64.5 us
  Pallas kernels  62.3 us (96%)
  local copies, waits for them, and re-layouts  1.54 us (2%)
  between operations  0.66 us (1%)
    pallas_call x1, Pallas kernels, on_device_fused(): pl.pallas_call(fused_kernel, out_shape=jax.ShapeDtypeStruct((SEQ_DEV, vis...  62.3 us
    unnamed x1, local copies, waits for them, and re-layouts  1.54 us

profile of v4, /device:TPU:0, one launch (start us, length us, event | category | flops | bytes accessed | tf_op | source)
XLA Modules:
  0.0 64.5 jit_solution(3674525641805665824)
XLA Ops:
  0.7 62.3 %shard_map.118 = bf16[96,448]{1,0:T(8,128)(2,1)} custom-call(bf16[128,128]{1,0:T(8,128)(2,1)} %fb.1, bf16[384,1280]{1,0:T(8,128)(2,1)} %conv_h.1, f32[1280]{0:T(1024)} %gain1.1, bf16[160,1280]{1,0:T(8,128)(2,1)} %up.1, bf16[160,1280]{1,0:T(8,128)(2,1)} %bitcast.6, f32[1280]{0:T(1024)} %gain2.1, bf16[448,1280]{1,0:T(8,128)(2,1)} %bitcast.4, ...), custom_call_target="tpu_custom_call" | custom-call | tf_op jit(solution)/shard_map/pallas_call | solution.py:479
  62.9 1.5 %copy.15 = bf16[1,96,448]{2,1,0:T(8,128)(2,1)} copy(bf16[1,96,448]{2,1,0:T(8,128)(2,1)} %bitcast.7) | data formatting | bytes 172032

commit v5 on v4

--- a/solution.py
+++ b/solution.py
@@ -164,7 +164,7 @@
 FB, META, UPW, DNW, MRG, VIS, TOT, FWD, NRM, HID, COR, XAX = 0, 7, 14, 21, 28, 35, 42, 56, 59, 62, 66, 68
 N_SEM = 70
 HALF = 640
-FLIPS = (4, 6, 5, 7, 2, 3, 1)
+SHIFTS = (4, 3, 5, 2, 6, 1, 7)
 
 
 def flipped(index, bits):
@@ -182,7 +182,8 @@
     me = lax.axis_index("tm")
     mo = lax.axis_index("mod")
     xx, cc = mo // 2, mo % 2
-    tm_peers = [flipped(me, bits) for bits in FLIPS]
+    tm_peers = [lax.rem(me + d, TM) for d in SHIFTS]
+    tm_sources = [lax.rem(me + TM - d, TM) for d in SHIFTS]
     mod_peers = [flipped(mo, bits) for bits in (2, 3, 1)]
     x_peer, core_peer = mod_peers[0], mod_peers[2]
 
@@ -263,7 +264,7 @@
         pl.when(jnp.logical_not(here))(lambda: act(1))
 
     fb_out = [frames(d, p, me) for d, p in enumerate(tm_peers)]
-    fb_in = [frames(d, p, p) for d, p in enumerate(tm_peers)]
+    fb_in = [frames(d, p, p) for d, p in enumerate(tm_sources)]
     pl.semaphore_wait(barrier, TM + MOD - 2)
     both_ways(me, lambda i: [c[i].start() for c in fb_out] and None)
     up_rows, dn_rows = pl.ds(0, 240), pl.ds(240, 160)
@@ -284,7 +285,7 @@
     d_copies = to_tm(lambda p: w_s.at[p, dn_rows], w_r.at[me, dn_rows], DNW)
 
     loads[1].wait()
-    for d, p in enumerate(tm_peers):
+    for d, p in enumerate(tm_sources):
         both_ways(p, lambda i: fb_in[d][i].wait_recv())
 
     def stem_step(first):
@@ -309,8 +310,10 @@
             arrive(m_copies)
             x_copies = [
                 copy(x_r.at[:, mo], x_r.at[:, mo], FWD + d, {"mod": p})
-                for d, p in enumerate(mod_peers)
+                for d, p in enumerate((x_peer, core_peer))
             ]
+    x_copies[0].wait_recv()
+    x_copies.append(copy(x_r.at[:, x_peer], x_r.at[:, x_peer], FWD + 2, {"mod": core_peer}))
 
     arrive(meta_copies)
     ends, before, running = [], [], jnp.zeros((1, 128), F32)
@@ -360,7 +363,7 @@
         pool = pool_rows(r128 // 16, (r128 // 8) % 2, r128 % 8, c128, ends_of(pair))
         pa[k] = mm(pool, act).astype(BF16)
 
-    arrive(x_copies)
+    arrive(x_copies[1:])
     lane = iota((1, 128), 1)
     pos = jnp.concatenate(
         [

time: 64.7 us -> 64.4 us (level)
  no operation moved by 1% of the time
where the time goes in v5:
time: 64.4 us; the launch traced here: 64.3 us
  Pallas kernels  62.1 us (96%)
  local copies, waits for them, and re-layouts  1.54 us (2%)
  between operations  0.66 us (1%)
    pallas_call x1, Pallas kernels, on_device_fused(): pl.pallas_call(fused_kernel, out_shape=jax.ShapeDtypeStruct((SEQ_DEV, vis...  62.1 us
    unnamed x1, local copies, waits for them, and re-layouts  1.54 us

profile of v5, /device:TPU:0, one launch (start us, length us, event | category | flops | bytes accessed | tf_op | source)
XLA Modules:
  0.0 64.3 jit_solution(18247137963390925430)
XLA Ops:
  0.7 62.1 %shard_map.118 = bf16[96,448]{1,0:T(8,128)(2,1)} custom-call(bf16[128,128]{1,0:T(8,128)(2,1)} %fb.1, bf16[384,1280]{1,0:T(8,128)(2,1)} %conv_h.1, f32[1280]{0:T(1024)} %gain1.1, bf16[160,1280]{1,0:T(8,128)(2,1)} %up.1, bf16[160,1280]{1,0:T(8,128)(2,1)} %bitcast.6, f32[1280]{0:T(1024)} %gain2.1, bf16[448,1280]{1,0:T(8,128)(2,1)} %bitcast.4, ...), custom_call_target="tpu_custom_call" | custom-call | tf_op jit(solution)/shard_map/pallas_call | solution.py:482
  62.7 1.5 %copy.15 = bf16[1,96,448]{2,1,0:T(8,128)(2,1)} copy(bf16[1,96,448]{2,1,0:T(8,128)(2,1)} %bitcast.7) | data formatting | bytes 172032

commit v6 on v5

--- a/solution.py
+++ b/solution.py
@@ -176,7 +176,7 @@
 
 def fused_kernel(
     fb, conv_h, gain1, up, dn, gain2, aud_h, pat_h, gain_v, vis_h, ret, kept, out,
-    conv, aud_w, pat, vis_w, fbp, meta, w_s, w_r, m_s, x_r, v_s, v_r, stem, hid, pa, own,
+    conv, aud_w, pat, vis_w, fbp, meta, w_s, w_r, m_s, x_r, v_s, v_r, pre, w_all, stem, hid, pa, own,
     a_s, a_r, b_s, b_r, c_s, c_r, nrm, load_sem, send_sem, recv_sem,
 ):
     me = lax.axis_index("tm")
@@ -205,11 +205,14 @@
 
     sent = []
 
-    def copy(src, dst, slot, to):
-        c = pltpu.make_async_remote_copy(
+    def describe(src, dst, slot, to):
+        return pltpu.make_async_remote_copy(
             src_ref=src, dst_ref=dst, send_sem=send_sem.at[slot], recv_sem=recv_sem.at[slot],
             device_id=to, device_id_type=MESH,
         )
+
+    def copy(src, dst, slot, to):
+        c = describe(src, dst, slot, to)
         c.start()
         sent.append(c)
         return c
@@ -288,30 +291,50 @@
     for d, p in enumerate(tm_sources):
         both_ways(p, lambda i: fb_in[d][i].wait_recv())
 
-    def stem_step(first):
-        base = pl.multiple_of(first * 128, 128)
+    def span_of(k):
+        x_at = (1 - xx) + (k // 2) * (2 * xx - 1)
+        return 2 * (2 * x_at + cc) + k % 2
+
+    def hidden_rows(k):
+        rows = pl.ds(pl.multiple_of(span_of(k) * 128, 128), 128)
+        return describe(hid.at[rows], hid.at[rows], HID + k, {"mod": core_peer})
+
+    x_copies = [
+        describe(x_r.at[:, mo], x_r.at[:, mo], FWD + d, {"mod": p})
+        for d, p in enumerate((x_peer, core_peer))
+    ]
+
+    def stem_step(k, carry):
+        base = pl.multiple_of(span_of(k) * 128, 128)
         rows = fbp[pl.ds(base, 160), :].astype(F32)
         taps = jnp.concatenate([rows[15:143], rows[16:144], rows[17:145]], axis=1).astype(BF16)
-        st = gelu(mm(taps, conv[...])).astype(BF16)
-        stem[pl.ds(base, 128), :] = st
-        v = st.astype(F32)
-        v = v - jnp.sum(v, axis=1, keepdims=True) * (1.0 / 1280.0)
-        var = jnp.sum(v * v, axis=1, keepdims=True) * (1.0 / 1280.0)
-        hid[pl.ds(base, 128), :] = (v * lax.rsqrt(var + 1e-05) * gain1[...][None, :]).astype(BF16)
-
-    h_copies = []
-    for k in range(4):
-        x_at = 1 - xx if k < 2 else xx
-        span = 2 * (2 * x_at + cc) + k % 2
-        stem_step(span)
-        rows = pl.ds(pl.multiple_of(span * 128, 128), 128)
-        h_copies.append(copy(hid.at[rows], hid.at[rows], HID + k, {"mod": core_peer}))
-        if k == 1:
+        pre[...] = mm(taps, conv[...])
+
+        def piece(i, carry):
+            at = pl.multiple_of(i * 32, 32)
+            st = gelu(pre[pl.ds(at, 32), :]).astype(BF16)
+            there = pl.ds(pl.multiple_of(base + at, 32), 32)
+            stem[there, :] = st
+            v = st.astype(F32)
+            v = v - jnp.sum(v, axis=1, keepdims=True) * (1.0 / 1280.0)
+            var = jnp.sum(v * v, axis=1, keepdims=True) * (1.0 / 1280.0)
+            hid[there, :] = (v * lax.rsqrt(var + 1e-05) * gain1[...][None, :]).astype(BF16)
+            return carry
+
+        lax.fori_loop(0, 4, piece, 0)
+        hidden_rows(k).start()
+
+        @pl.when(k == 1)
+        def _():
             arrive(m_copies)
-            x_copies = [
-                copy(x_r.at[:, mo], x_r.at[:, mo], FWD + d, {"mod": p})
-                for d, p in enumerate((x_peer, core_peer))
-            ]
+            for c in x_copies:
+                c.start()
+
+        return carry
+
+    lax.fori_loop(0, 4, stem_step, 0)
+    h_copies = [hidden_rows(k) for k in range(4)]
+    sent.extend(h_copies + x_copies)
     x_copies[0].wait_recv()
     x_copies.append(copy(x_r.at[:, x_peer], x_r.at[:, x_peer], FWD + 2, {"mod": core_peer}))
 
@@ -351,17 +374,23 @@
             parts.append(rem[80 * t : 80 * t + 80, lane + 128 : lane + 256])
         return jnp.concatenate([main, jnp.concatenate(parts, axis=0)], axis=1)
 
-    up_all = assemble(0, 0)
+    w_all[...] = assemble(0, 0)
     r128, c128 = iota((128, 128), 0), iota((128, 128), 1)
-    order = [(1 - cc, 1 - xx), (1 - cc, xx), (cc, 1 - xx), (cc, xx)]
-    for k in (2, 0, 3, 1):
-        if k < 2:
-            arrive(h_copies[2 * k : 2 * k + 2])
-        pair = 2 * order[k][1] + order[k][0]
+
+    def feed(step, carry):
+        k = lax.rem(2 + 2 * step + step // 2, 4)
+        core = (1 - cc) + (k // 2) * (2 * cc - 1)
+        x_at = (1 - xx) + (k % 2) * (2 * xx - 1)
+        pl.when(step == 1)(lambda: arrive(h_copies[0:2]))
+        pl.when(step == 3)(lambda: arrive(h_copies[2:4]))
+        pair = 2 * x_at + core
         rows = pl.ds(pl.multiple_of(pair * 256, 256), 256)
-        act = gelu(mm(hid[rows, :], up_all)).astype(BF16)
+        act = gelu(mm(hid[rows, :], w_all[...])).astype(BF16)
         pool = pool_rows(r128 // 16, (r128 // 8) % 2, r128 % 8, c128, ends_of(pair))
         pa[k] = mm(pool, act).astype(BF16)
+        return carry
+
+    lax.fori_loop(0, 4, feed, 0)
 
     arrive(x_copies[1:])
     lane = iota((1, 128), 1)
@@ -381,17 +410,34 @@
     v_r[me] = v_s[me]
 
     arrive(d_copies)
-    dn_all = assemble(240, 256)
-    a_copies, b_copies, c_copies = [], [], []
-    for h in range(2):
-        product = mm_nt(pa[...].reshape(512, 256), dn_all[HALF * h : HALF * h + HALF])
+    w_all[...] = assemble(240, 256)
+
+    def core_sum(h):
+        return describe(a_s.at[h], a_r.at[h], COR + h, {"mod": core_peer})
+
+    def x_sum(h):
+        return describe(b_s.at[h], b_r.at[h], XAX + h, {"mod": x_peer})
+
+    def product_half(h, carry):
+        cols = pl.ds(pl.multiple_of(h * HALF, HALF), HALF)
+        product = mm_nt(pa[...].reshape(512, 256), w_all[cols, :])
         a_s[h] = product[0:256].astype(BF16)
-        a_copies.append(copy(a_s.at[h], a_r.at[h], COR + h, {"mod": core_peer}))
+        core_sum(h).start()
         own[h] = product[256:512]
-    for h in range(2):
-        a_copies[h].wait_recv()
+        return carry
+
+    lax.fori_loop(0, 2, product_half, 0)
+
+    def x_half(h, carry):
+        core_sum(h).wait_recv()
         b_s[h] = (own[h, 0:128] + a_r[h, 0:128].astype(F32)).astype(BF16)
-        b_copies.append(copy(b_s.at[h], b_r.at[h], XAX + h, {"mod": x_peer}))
+        x_sum(h).start()
+        return carry
+
+    lax.fori_loop(0, 2, x_half, 0)
+    b_copies = [x_sum(h) for h in range(2)]
+    sent.extend([core_sum(h) for h in range(2)] + b_copies)
+    c_copies = []
 
     r16, c16 = iota((16, 128), 0), iota((16, 128), 1)
     pool = pool_rows(me, r16 // 8, r16 % 8, c16, ends_of(mo))
@@ -464,6 +510,8 @@
         pltpu.VMEM((TM, MOD, 16, HALF), BF16),
         pltpu.VMEM((TM, 32, n_out), BF16),
         pltpu.VMEM((TM, 32, n_out), BF16),
+        pltpu.VMEM((128, 1280), F32),
+        pltpu.VMEM((1280, 256), BF16),
         pltpu.VMEM((1024, 1280), BF16),
         pltpu.VMEM((1024, 1280), BF16),
         pltpu.VMEM((MOD, 128, 256), BF16),

time: 64.4 us -> 64.4 us (level)
  no operation moved by 1% of the time
where the time goes in v6:
time: 64.4 us; the launch traced here: 64.2 us
  Pallas kernels  62 us (96%)
  local copies, waits for them, and re-layouts  1.54 us (2%)
  between operations  0.66 us (1%)
    pallas_call x1, Pallas kernels, on_device_fused(): pl.pallas_call(fused_kernel, out_shape=jax.ShapeDtypeStruct((SEQ_DEV, vis...  62 us
    unnamed x1, local copies, waits for them, and re-layouts  1.54 us

profile of v6, /device:TPU:0, one launch (start us, length us, event | category | flops | bytes accessed | tf_op | source)
XLA Modules:
  0.0 64.2 jit_solution(12878913645104122059)
XLA Ops:
  0.7 62.0 %shard_map.118 = bf16[96,448]{1,0:T(8,128)(2,1)} custom-call(bf16[128,128]{1,0:T(8,128)(2,1)} %fb.1, bf16[384,1280]{1,0:T(8,128)(2,1)} %conv_h.1, f32[1280]{0:T(1024)} %gain1.1, bf16[160,1280]{1,0:T(8,128)(2,1)} %up.1, bf16[160,1280]{1,0:T(8,128)(2,1)} %bitcast.6, f32[1280]{0:T(1024)} %gain2.1, bf16[448,1280]{1,0:T(8,128)(2,1)} %bitcast.4, ...), custom_call_target="tpu_custom_call" | custom-call | tf_op jit(solution)/shard_map/pallas_call | solution.py:530
  62.7 1.5 %copy.15 = bf16[1,96,448]{2,1,0:T(8,128)(2,1)} copy(bf16[1,96,448]{2,1,0:T(8,128)(2,1)} %bitcast.7) | data formatting | bytes 172032

commit v7 on v6

--- a/solution.py
+++ b/solution.py
@@ -157,8 +157,31 @@
     return lax.dot_general(a, b, (((0,), (0,)), ((), ())), preferred_element_type=F32)
 
 
+ERF_TOP = (
+    -2.72614225801306e-10, 2.77068142495902e-08, -2.10102402082508e-06, -5.69250639462346e-05,
+    -7.34990630326855e-04, -2.95459980854025e-03, -1.60960333262415e-02,
+)
+ERF_BOTTOM = (
+    -1.45660718464996e-05, -2.13374055278905e-04, -1.68282697438203e-03, -7.37332916720468e-03,
+    -1.42647390514189e-02,
+)
+
+
+def polynomial(x, terms):
+    value = jnp.full_like(x, terms[0])
+    for term in terms[1:]:
+        value = value * x + term
+    return value
+
+
+def erf(x):
+    x = jnp.clip(x, -4.0, 4.0)
+    square = x * x
+    return x * polynomial(square, ERF_TOP) / polynomial(square, ERF_BOTTOM)
+
+
 def gelu(x):
-    return 0.5 * x * (1.0 + lax.erf(x * 0.7071067811865476))
+    return 0.5 * x * (1.0 + erf(x * 0.7071067811865476))
 
 
 FB, META, UPW, DNW, MRG, VIS, TOT, FWD, NRM, HID, COR, XAX = 0, 7, 14, 21, 28, 35, 42, 56, 59, 62, 66, 68
@@ -304,6 +327,8 @@
         for d, p in enumerate((x_peer, core_peer))
     ]
 
+    gain_row = gain1[...][None, :]
+
     def stem_step(k, carry):
         base = pl.multiple_of(span_of(k) * 128, 128)
         rows = fbp[pl.ds(base, 160), :].astype(F32)
@@ -318,7 +343,7 @@
             v = st.astype(F32)
             v = v - jnp.sum(v, axis=1, keepdims=True) * (1.0 / 1280.0)
             var = jnp.sum(v * v, axis=1, keepdims=True) * (1.0 / 1280.0)
-            hid[there, :] = (v * lax.rsqrt(var + 1e-05) * gain1[...][None, :]).astype(BF16)
+            hid[there, :] = (v * lax.rsqrt(var + 1e-05) * gain_row).astype(BF16)
             return carry
 
         lax.fori_loop(0, 4, piece, 0)

time: 64.4 us -> 65.2 us (1.012)
  Pallas kernels: 62 us -> 62.8 us
    pallas_call x1, Pallas kernels: 62 us -> 62.8 us  [on_device_fused(): pl.pallas_call(fused_kernel, out_shape=jax.ShapeDtypeStruct((SEQ_DEV, vis...]
where the time goes in v7:
time: 65.2 us; the launch traced here: 65 us
  Pallas kernels  62.8 us (96%)
  local copies, waits for them, and re-layouts  1.54 us (2%)
  between operations  0.66 us (1%)
    pallas_call x1, Pallas kernels, on_device_fused(): pl.pallas_call(fused_kernel, out_shape=jax.ShapeDtypeStruct((SEQ_DEV, vis...  62.8 us
    unnamed x1, local copies, waits for them, and re-layouts  1.54 us

profile of v7, /device:TPU:0, one launch (start us, length us, event | category | flops | bytes accessed | tf_op | source)
XLA Modules:
  0.0 65.0 jit_solution(1049811988748044378)
XLA Ops:
  0.7 62.8 %shard_map.118 = bf16[96,448]{1,0:T(8,128)(2,1)} custom-call(bf16[128,128]{1,0:T(8,128)(2,1)} %fb.1, bf16[384,1280]{1,0:T(8,128)(2,1)} %conv_h.1, f32[1280]{0:T(1024)} %gain1.1, bf16[160,1280]{1,0:T(8,128)(2,1)} %up.1, bf16[160,1280]{1,0:T(8,128)(2,1)} %bitcast.6, f32[1280]{0:T(1024)} %gain2.1, bf16[448,1280]{1,0:T(8,128)(2,1)} %bitcast.4, ...), custom_call_target="tpu_custom_call" | custom-call | tf_op jit(solution)/shard_map/pallas_call | solution.py:555
  63.5 1.5 %copy.15 = bf16[1,96,448]{2,1,0:T(8,128)(2,1)} copy(bf16[1,96,448]{2,1,0:T(8,128)(2,1)} %bitcast.7) | data formatting | bytes 172032

commit v8 on v6

--- a/solution.py
+++ b/solution.py
@@ -161,8 +161,9 @@
     return 0.5 * x * (1.0 + lax.erf(x * 0.7071067811865476))
 
 
-FB, META, UPW, DNW, MRG, VIS, TOT, FWD, NRM, HID, COR, XAX = 0, 7, 14, 21, 28, 35, 42, 56, 59, 62, 66, 68
-N_SEM = 70
+FB, META, UPW, DNW, MRG, VIS, TOT, FWD, NRM, HID, COR, XAX = 0, 7, 14, 21, 28, 35, 42, 77, 80, 83, 87, 92
+N_SEM = 97
+CHUNKS, WIDE = 5, 256
 HALF = 640
 SHIFTS = (4, 3, 5, 2, 6, 1, 7)
 
@@ -419,14 +420,14 @@
         return describe(b_s.at[h], b_r.at[h], XAX + h, {"mod": x_peer})
 
     def product_half(h, carry):
-        cols = pl.ds(pl.multiple_of(h * HALF, HALF), HALF)
+        cols = pl.ds(pl.multiple_of(h * WIDE, WIDE), WIDE)
         product = mm_nt(pa[...].reshape(512, 256), w_all[cols, :])
         a_s[h] = product[0:256].astype(BF16)
         core_sum(h).start()
         own[h] = product[256:512]
         return carry
 
-    lax.fori_loop(0, 2, product_half, 0)
+    lax.fori_loop(0, CHUNKS, product_half, 0)
 
     def x_half(h, carry):
         core_sum(h).wait_recv()
@@ -434,9 +435,9 @@
         x_sum(h).start()
         return carry
 
-    lax.fori_loop(0, 2, x_half, 0)
-    b_copies = [x_sum(h) for h in range(2)]
-    sent.extend([core_sum(h) for h in range(2)] + b_copies)
+    lax.fori_loop(0, CHUNKS, x_half, 0)
+    b_copies = [x_sum(h) for h in range(CHUNKS)]
+    sent.extend([core_sum(h) for h in range(CHUNKS)] + b_copies)
     c_copies = []
 
     r16, c16 = iota((16, 128), 0), iota((16, 128), 1)
@@ -452,11 +453,11 @@
     slot = jnp.where(lane < 32, v_slot, jnp.where(lane < 96, a_slot, -1))
     place = onehot(slot == iota((96, 128), 0))
 
-    for h in range(2):
+    for h in range(CHUNKS):
         total = own[h, 128:256] + a_r[h, 128:256].astype(F32)
         b_copies[h].wait_recv()
         total = total + b_r[h].astype(F32)
-        c_s[h] = total.astype(BF16).reshape(TM, 16, HALF)
+        c_s[h] = total.astype(BF16).reshape(TM, 16, WIDE)
         c_copies.append(to_tm(lambda p: c_s.at[h, p], c_r.at[h, me], TOT + 7 * h))
         c_r[h, me] = c_s[h, me]
 
@@ -466,9 +467,9 @@
         visual = visual + v_r[t].astype(F32)
 
     halves = []
-    for h in range(2):
+    for h in range(CHUNKS):
         arrive(c_copies[h])
-        part = pooled[:, HALF * h : HALF * h + HALF]
+        part = pooled[:, WIDE * h : WIDE * h + WIDE]
         for t in range(TM):
             part = part + c_r[h, t].astype(F32)
         halves.append(part)
@@ -515,13 +516,13 @@
         pltpu.VMEM((1024, 1280), BF16),
         pltpu.VMEM((1024, 1280), BF16),
         pltpu.VMEM((MOD, 128, 256), BF16),
-        pltpu.VMEM((2, 256, HALF), F32),
-        pltpu.VMEM((2, 256, HALF), BF16),
-        pltpu.VMEM((2, 256, HALF), BF16),
-        pltpu.VMEM((2, 128, HALF), BF16),
-        pltpu.VMEM((2, 128, HALF), BF16),
-        pltpu.VMEM((2, TM, 16, HALF), BF16),
-        pltpu.VMEM((2, TM, 16, HALF), BF16),
+        pltpu.VMEM((CHUNKS, 256, WIDE), F32),
+        pltpu.VMEM((CHUNKS, 256, WIDE), BF16),
+        pltpu.VMEM((CHUNKS, 256, WIDE), BF16),
+        pltpu.VMEM((CHUNKS, 128, WIDE), BF16),
+        pltpu.VMEM((CHUNKS, 128, WIDE), BF16),
+        pltpu.VMEM((CHUNKS, TM, 16, WIDE), BF16),
+        pltpu.VMEM((CHUNKS, TM, 16, WIDE), BF16),
         pltpu.VMEM((MOD, 16, 1280), BF16),
         pltpu.SemaphoreType.DMA((4,)),
         pltpu.SemaphoreType.DMA((N_SEM,)),

time: 64.4 us -> 63.1 us (0.980)
  Pallas kernels: 62 us -> 60.8 us
    pallas_call x1, Pallas kernels: 62 us -> 60.8 us  [on_device_fused(): pl.pallas_call(fused_kernel, out_shape=jax.ShapeDtypeStruct((SEQ_DEV, vis...]
where the time goes in v8:
time: 63.1 us; the launch traced here: 63 us
  Pallas kernels  60.8 us (96%)
  local copies, waits for them, and re-layouts  1.54 us (2%)
  between operations  0.66 us (1%)
    pallas_call x1, Pallas kernels, on_device_fused(): pl.pallas_call(fused_kernel, out_shape=jax.ShapeDtypeStruct((SEQ_DEV, vis...  60.8 us
    unnamed x1, local copies, waits for them, and re-layouts  1.54 us

profile of v8, /device:TPU:0, one launch (start us, length us, event | category | flops | bytes accessed | tf_op | source)
XLA Modules:
  0.0 63.0 jit_solution(1806195641289936608)
XLA Ops:
  0.7 60.8 %shard_map.118 = bf16[96,448]{1,0:T(8,128)(2,1)} custom-call(bf16[128,128]{1,0:T(8,128)(2,1)} %fb.1, bf16[384,1280]{1,0:T(8,128)(2,1)} %conv_h.1, f32[1280]{0:T(1024)} %gain1.1, bf16[160,1280]{1,0:T(8,128)(2,1)} %up.1, bf16[160,1280]{1,0:T(8,128)(2,1)} %bitcast.6, f32[1280]{0:T(1024)} %gain2.1, bf16[448,1280]{1,0:T(8,128)(2,1)} %bitcast.4, ...), custom_call_target="tpu_custom_call" | custom-call | tf_op jit(solution)/shard_map/pallas_call | solution.py:531
  61.4 1.5 %copy.15 = bf16[1,96,448]{2,1,0:T(8,128)(2,1)} copy(bf16[1,96,448]{2,1,0:T(8,128)(2,1)} %bitcast.7) | data formatting | bytes 172032

commit v9 on v8

--- a/solution.py
+++ b/solution.py
@@ -427,15 +427,19 @@
         own[h] = product[256:512]
         return carry
 
-    lax.fori_loop(0, CHUNKS, product_half, 0)
-
     def x_half(h, carry):
         core_sum(h).wait_recv()
         b_s[h] = (own[h, 0:128] + a_r[h, 0:128].astype(F32)).astype(BF16)
         x_sum(h).start()
         return carry
 
-    lax.fori_loop(0, CHUNKS, x_half, 0)
+    def both(h, carry):
+        product_half(h, carry)
+        return x_half(h - 1, carry)
+
+    product_half(0, 0)
+    lax.fori_loop(1, CHUNKS, both, 0)
+    x_half(CHUNKS - 1, 0)
     b_copies = [x_sum(h) for h in range(CHUNKS)]
     sent.extend([core_sum(h) for h in range(CHUNKS)] + b_copies)
     c_copies = []

time: 63.1 us -> 63 us (level)
  no operation moved by 1% of the time
where the time goes in v9:
time: 63 us; the launch traced here: 62.8 us
  Pallas kernels  60.6 us (96%)
  local copies, waits for them, and re-layouts  1.54 us (2%)
  between operations  0.66 us (1%)
    pallas_call x1, Pallas kernels, on_device_fused(): pl.pallas_call(fused_kernel, out_shape=jax.ShapeDtypeStruct((SEQ_DEV, vis...  60.6 us
    unnamed x1, local copies, waits for them, and re-layouts  1.54 us

profile of v9, /device:TPU:0, one launch (start us, length us, event | category | flops | bytes accessed | tf_op | source)
XLA Modules:
  0.0 62.8 jit_solution(7134078507956715443)
XLA Ops:
  0.7 60.6 %shard_map.118 = bf16[96,448]{1,0:T(8,128)(2,1)} custom-call(bf16[128,128]{1,0:T(8,128)(2,1)} %fb.1, bf16[384,1280]{1,0:T(8,128)(2,1)} %conv_h.1, f32[1280]{0:T(1024)} %gain1.1, bf16[160,1280]{1,0:T(8,128)(2,1)} %up.1, bf16[160,1280]{1,0:T(8,128)(2,1)} %bitcast.6, f32[1280]{0:T(1024)} %gain2.1, bf16[448,1280]{1,0:T(8,128)(2,1)} %bitcast.4, ...), custom_call_target="tpu_custom_call" | custom-call | tf_op jit(solution)/shard_map/pallas_call | solution.py:535
  61.3 1.5 %copy.15 = bf16[1,96,448]{2,1,0:T(8,128)(2,1)} copy(bf16[1,96,448]{2,1,0:T(8,128)(2,1)} %bitcast.7) | data formatting | bytes 172032
